TPU v7x, 512 devices: a whole 4x4x16 slice. The times are simulated.
512 devices in a mesh: slab: 128 (over y, z, core), sub: 4 (over x).
Axes of the slice: x: 4, y: 4, z: 16, core: 2. Of those that a mesh axis runs over, the one named last changes fastest.
Arguments:
- adjoint: float32 [80, 262144], P(None, ('slab', 'sub')), may hold values from -6 to 6
- elem_scale: float32 [262144], P(('slab', 'sub')), may hold values from 0.5 to 2
- cluster: int32 [262144], P(('slab', 'sub')), may hold values from 0 to 2
- face_links: int32 [4, 262144], P(None, ('slab', 'sub')), may hold values from 0 to 1023
- halo_list: int32 [2, 131072], P(None, ('slab', 'sub')), may hold values from 0 to 511, as said below
- k_matrix: float32 [80, 80], replicated, may hold values from -0.625 to 0.625
- w_self: float32 [80, 80], replicated, may hold values from -0.625 to 0.625
- w_neighbour: float32 [80, 320], replicated, may hold values from -0.3125 to 0.3125
Outputs:
- result: float32 [80, 262144], P(None, ('slab', 'sub'))
Inputs may be any that keep to these rules, and one draw needn't show every extreme that they name: `face_links`: on each device, a value below 512 names its own element; 512 + k names slot k of the received halo columns in the order of the steps. `halo_list`: on each device the 512 listed elements are distinct; each of the four sides of 128 listed elements holds at most 48 elements of any one cluster, and exactly 48 of two clusters.
All inputs are finite; a program needn't handle non-finite values.
Results may differ from a plain program's by a relative error of at most 0.0001.
Values sent between devices are 32-bit elements; how exact they have to be, the bound alone decides.
A program may use at most 64 MiB of HBM per device.

v0:
```python
import jax
import jax.numpy as jnp
from jax import lax
from jax.sharding import PartitionSpec as P

time_step = 0.125


def with_halo(cells, sides, width):
    for axis, dim in sides:
        count = lax.axis_size(axis)
        ends = count - 1
        head = lax.slice_in_dim(cells, 0, width, axis=dim)
        tail = lax.slice_in_dim(cells, cells.shape[dim] - width, cells.shape[dim], axis=dim)
        cells = jnp.concatenate(
            [
                lax.ppermute(tail, axis, [(i, (i + 1) % count) for i in range(ends)]),
                cells,
                lax.ppermute(head, axis, [((i + 1) % count, i) for i in range(ends)]),
            ],
            axis=dim,
        )
    return cells


def predict(source, scale_row, k_matrix, step_size):
    total = source
    current = source
    for degree in range(1, 4):
        current = (
            step_size
            / (degree + 1)
            * scale_row
            * jnp.dot(k_matrix, current, precision=lax.Precision.HIGHEST)
        )
        total = total + current
    return total


def outer_cols(slab_got, sub_got, halo_width):
    return jnp.concatenate(
        [
            slab_got[:, :halo_width],
            slab_got[:, 3 * halo_width :],
            sub_got[:, :halo_width],
            sub_got[:, 3 * halo_width :],
        ],
        axis=1,
    )


def shards(adjoint, elem_scale, cluster, face_links, halo_list, k_matrix, w_self, w_neighbour):
    halo_width = halo_list.shape[1] // 2
    scale_row = elem_scale[None, :]
    for substep in (3, 2, 1, 0):
        for rate_level in (2, 1, 0):
            if (substep + 1) % 2**rate_level == 0:
                step_size = time_step * 2.0**rate_level
                active = (cluster == rate_level).astype(jnp.float32)[None, :]
                masked = adjoint * active
                predicted = predict(masked, scale_row, k_matrix, step_size)
                slab_got = with_halo(
                    jnp.take(predicted, halo_list[0], axis=1), (("slab", 1),), halo_width
                )
                sub_got = with_halo(
                    jnp.take(predicted, halo_list[1], axis=1), (("sub", 1),), halo_width
                )
                far_cols = outer_cols(slab_got, sub_got, halo_width)
                extended = jnp.concatenate([predicted, far_cols], axis=1)
                stacked = jnp.concatenate(
                    [jnp.take(extended, face_links[face_id], axis=1) for face_id in range(4)],
                    axis=0,
                )
                coupled = jnp.dot(w_neighbour, stacked, precision=lax.Precision.HIGHEST)
                change = scale_row * (
                    jnp.dot(w_self, predicted, precision=lax.Precision.HIGHEST) + coupled
                )
                adjoint = adjoint + step_size * change
    return adjoint


def solution(mesh):
    placed = (
        P(None, ("slab", "sub")),
        P(("slab", "sub")),
        P(("slab", "sub")),
        P(None, ("slab", "sub")),
        P(None, ("slab", "sub")),
        P(),
        P(),
        P(),
    )
    return jax.shard_map(
        shards, mesh=mesh, in_specs=placed, out_specs=P(None, ("slab", "sub")), check_vma=False
    )
```

profile of v0, /device:TPU:24, one launch (start us, length us, event | category | flops | bytes accessed | tf_op | source)
XLA Modules:
  0.0 181.6 jit_solution(5717664302326053119)
XLA Ops:
  2.2 1.2 convolution_multiply_fusion.20
  5.6 1.3 collective-permute-start.3
  6.9 4.5 %collective-permute-start.2 = (f32[80,128]{1,0:T(8,128)S(1)}, f32[80,128]{1,0:T(8,128)S(1)}, u32[]{:S(2)}, u32[]{:S(2)}) collective-permute-start(f32[80,128]{1,0:T(8,128)S(1)} %get-tuple-element.32), channel_id=1, source_target_pairs={{0,1},{1,2},{2,3},{4,5},{5,6},{6,7},{8,9},{9,10},{10,11},{12,13},{... | collective-permute-start | bytes 122888 | tf_op jit(solution)/shard_map/ppermute | solution.py:17
  12.4 10.5 %collective-permute-start.1 = (f32[80,128]{1,0:T(8,128)S(1)}, f32[80,128]{1,0:T(8,128)S(1)}, u32[]{:S(2)}, u32[]{:S(2)}) collective-permute-start(f32[80,128]{1,0:T(8,128)S(1)} %get-tuple-element.33), channel_id=1, source_target_pairs={{4,0},{8,4},{12,8},{16,12},{20,16},{24,20},{28,24},{32,28},{36,32}... | collective-permute-start | bytes 122888 | tf_op jit(solution)/shard_map/ppermute | solution.py:19
  22.8 1.9 %collective-permute-start = (f32[80,128]{1,0:T(8,128)S(1)}, f32[80,128]{1,0:T(8,128)S(1)}, u32[]{:S(2)}, u32[]{:S(2)}) collective-permute-start(f32[80,128]{1,0:T(8,128)S(1)} %get-tuple-element.34), channel_id=1, source_target_pairs={{0,4},{4,8},{8,12},{12,16},{16,20},{20,24},{24,28},{28,32},{32,36}... | collective-permute-start | bytes 122888 | tf_op jit(solution)/shard_map/ppermute | solution.py:17
  25.2 5.0 %collective-permute-done = f32[80,128]{1,0:T(8,128)S(1)} collective-permute-done((f32[80,128]{1,0:T(8,128)S(1)}, f32[80,128]{1,0:T(8,128)S(1)}, u32[]{:S(2)}, u32[]{:S(2)}) %collective-permute-start) | collective-permute-done | bytes 40992 | tf_op jit(solution)/shard_map/ppermute | solution.py:17
  30.6 1.0 gather_fusion.5
  31.6 1.0 gather_fusion.4
  32.6 1.0 gather_fusion.3
  33.7 1.0 gather_fusion.2
  35.8 1.2 fusion.27
  40.1 1.9 %collective-permute-start.4 = (f32[80,128]{1,0:T(8,128)S(1)}, f32[80,128]{1,0:T(8,128)S(1)}, u32[]{:S(2)}, u32[]{:S(2)}) collective-permute-start(f32[80,128]{1,0:T(8,128)S(1)} %get-tuple-element.30), channel_id=1, source_target_pairs={{0,4},{4,8},{8,12},{12,16},{16,20},{20,24},{24,28},{28,32},{32,36}... | collective-permute-start | bytes 122888 | tf_op jit(solution)/shard_map/ppermute | solution.py:17
  42.1 1.3 collective-permute-start.7
  43.4 4.5 %collective-permute-start.6 = (f32[80,128]{1,0:T(8,128)S(1)}, f32[80,128]{1,0:T(8,128)S(1)}, u32[]{:S(2)}, u32[]{:S(2)}) collective-permute-start(f32[80,128]{1,0:T(8,128)S(1)} %get-tuple-element.28), channel_id=1, source_target_pairs={{0,1},{1,2},{2,3},{4,5},{5,6},{6,7},{8,9},{9,10},{10,11},{12,13},{... | collective-permute-start | bytes 122888 | tf_op jit(solution)/shard_map/ppermute | solution.py:17
  47.9 5.2 %collective-permute-start.5 = (f32[80,128]{1,0:T(8,128)S(1)}, f32[80,128]{1,0:T(8,128)S(1)}, u32[]{:S(2)}, u32[]{:S(2)}) collective-permute-start(f32[80,128]{1,0:T(8,128)S(1)} %get-tuple-element.29), channel_id=1, source_target_pairs={{4,0},{8,4},{12,8},{16,12},{20,16},{24,20},{28,24},{32,28},{36,32}... | collective-permute-start | bytes 122888 | tf_op jit(solution)/shard_map/ppermute | solution.py:19
  53.2 1.6 collective-permute-done.5
  55.0 1.0 gather_fusion.11
  56.1 1.0 gather_fusion.10
  57.1 1.0 gather_fusion.9
  58.2 1.0 gather_fusion.8
  59.8 1.2 fusion.24
  64.1 1.9 %collective-permute-start.8 = (f32[80,128]{1,0:T(8,128)S(1)}, f32[80,128]{1,0:T(8,128)S(1)}, u32[]{:S(2)}, u32[]{:S(2)}) collective-permute-start(f32[80,128]{1,0:T(8,128)S(1)} %get-tuple-element.26), channel_id=1, source_target_pairs={{0,4},{4,8},{8,12},{12,16},{16,20},{20,24},{24,28},{28,32},{32,36}... | collective-permute-start | bytes 122888 | tf_op jit(solution)/shard_map/ppermute | solution.py:17
  66.0 1.3 collective-permute-start.11
  67.3 4.5 %collective-permute-start.10 = (f32[80,128]{1,0:T(8,128)S(1)}, f32[80,128]{1,0:T(8,128)S(1)}, u32[]{:S(2)}, u32[]{:S(2)}) collective-permute-start(f32[80,128]{1,0:T(8,128)S(1)} %get-tuple-element.24), channel_id=1, source_target_pairs={{0,1},{1,2},{2,3},{4,5},{5,6},{6,7},{8,9},{9,10},{10,11},{12,13},{... | collective-permute-start | bytes 122888 | tf_op jit(solution)/shard_map/ppermute | solution.py:17
  71.9 5.4 %collective-permute-start.9 = (f32[80,128]{1,0:T(8,128)S(1)}, f32[80,128]{1,0:T(8,128)S(1)}, u32[]{:S(2)}, u32[]{:S(2)}) collective-permute-start(f32[80,128]{1,0:T(8,128)S(1)} %get-tuple-element.25), channel_id=1, source_target_pairs={{4,0},{8,4},{12,8},{16,12},{20,16},{24,20},{28,24},{32,28},{36,32}... | collective-permute-start | bytes 122888 | tf_op jit(solution)/shard_map/ppermute | solution.py:19
  77.3 1.4 collective-permute-done.9
  79.0 1.0 gather_fusion.17
  80.1 1.0 gather_fusion.16
  81.1 1.0 gather_fusion.15
  82.1 1.0 gather_fusion.14
  83.8 1.2 fusion.21
  88.1 1.9 %collective-permute-start.12 = (f32[80,128]{1,0:T(8,128)S(1)}, f32[80,128]{1,0:T(8,128)S(1)}, u32[]{:S(2)}, u32[]{:S(2)}) collective-permute-start(f32[80,128]{1,0:T(8,128)S(1)} %get-tuple-element.22), channel_id=1, source_target_pairs={{0,4},{4,8},{8,12},{12,16},{16,20},{20,24},{24,28},{28,32},{32,36}... | collective-permute-start | bytes 122888 | tf_op jit(solution)/shard_map/ppermute | solution.py:17
  90.0 1.3 collective-permute-start.15
  91.3 4.5 %collective-permute-start.14 = (f32[80,128]{1,0:T(8,128)S(1)}, f32[80,128]{1,0:T(8,128)S(1)}, u32[]{:S(2)}, u32[]{:S(2)}) collective-permute-start(f32[80,128]{1,0:T(8,128)S(1)} %get-tuple-element.20), channel_id=1, source_target_pairs={{0,1},{1,2},{2,3},{4,5},{5,6},{6,7},{8,9},{9,10},{10,11},{12,13},{... | collective-permute-start | bytes 122888 | tf_op jit(solution)/shard_map/ppermute | solution.py:17
  95.9 5.2 %collective-permute-start.13 = (f32[80,128]{1,0:T(8,128)S(1)}, f32[80,128]{1,0:T(8,128)S(1)}, u32[]{:S(2)}, u32[]{:S(2)}) collective-permute-start(f32[80,128]{1,0:T(8,128)S(1)} %get-tuple-element.21), channel_id=1, source_target_pairs={{4,0},{8,4},{12,8},{16,12},{20,16},{24,20},{28,24},{32,28},{36,32}... | collective-permute-start | bytes 122888 | tf_op jit(solution)/shard_map/ppermute | solution.py:19
  101.1 1.6 collective-permute-done.13
  103.0 1.0 gather_fusion.23
  104.0 1.0 gather_fusion.22
  105.1 1.0 gather_fusion.21
  106.1 1.0 gather_fusion.20
  107.7 1.2 fusion.18
  112.0 1.9 %collective-permute-start.16 = (f32[80,128]{1,0:T(8,128)S(1)}, f32[80,128]{1,0:T(8,128)S(1)}, u32[]{:S(2)}, u32[]{:S(2)}) collective-permute-start(f32[80,128]{1,0:T(8,128)S(1)} %get-tuple-element.18), channel_id=1, source_target_pairs={{0,4},{4,8},{8,12},{12,16},{16,20},{20,24},{24,28},{28,32},{32,36}... | collective-permute-start | bytes 122888 | tf_op jit(solution)/shard_map/ppermute | solution.py:17
  114.0 1.3 collective-permute-start.19
  115.3 4.5 %collective-permute-start.18 = (f32[80,128]{1,0:T(8,128)S(1)}, f32[80,128]{1,0:T(8,128)S(1)}, u32[]{:S(2)}, u32[]{:S(2)}) collective-permute-start(f32[80,128]{1,0:T(8,128)S(1)} %get-tuple-element.16), channel_id=1, source_target_pairs={{0,1},{1,2},{2,3},{4,5},{5,6},{6,7},{8,9},{9,10},{10,11},{12,13},{... | collective-permute-start | bytes 122888 | tf_op jit(solution)/shard_map/ppermute | solution.py:17
  119.8 5.2 %collective-permute-start.17 = (f32[80,128]{1,0:T(8,128)S(1)}, f32[80,128]{1,0:T(8,128)S(1)}, u32[]{:S(2)}, u32[]{:S(2)}) collective-permute-start(f32[80,128]{1,0:T(8,128)S(1)} %get-tuple-element.17), channel_id=1, source_target_pairs={{4,0},{8,4},{12,8},{16,12},{20,16},{24,20},{28,24},{32,28},{36,32}... | collective-permute-start | bytes 122888 | tf_op jit(solution)/shard_map/ppermute | solution.py:19
  125.1 1.6 collective-permute-done.17
  126.9 1.0 gather_fusion.29
  129.0 1.0 gather_fusion.27
  131.7 1.2 fusion.15
  136.0 1.9 %collective-permute-start.20 = (f32[80,128]{1,0:T(8,128)S(1)}, f32[80,128]{1,0:T(8,128)S(1)}, u32[]{:S(2)}, u32[]{:S(2)}) collective-permute-start(f32[80,128]{1,0:T(8,128)S(1)} %get-tuple-element.14), channel_id=1, source_target_pairs={{0,4},{4,8},{8,12},{12,16},{16,20},{20,24},{24,28},{28,32},{32,36}... | collective-permute-start | bytes 122888 | tf_op jit(solution)/shard_map/ppermute | solution.py:17
  137.9 1.3 collective-permute-start.23
  139.2 4.5 %collective-permute-start.22 = (f32[80,128]{1,0:T(8,128)S(1)}, f32[80,128]{1,0:T(8,128)S(1)}, u32[]{:S(2)}, u32[]{:S(2)}) collective-permute-start(f32[80,128]{1,0:T(8,128)S(1)} %get-tuple-element.12), channel_id=1, source_target_pairs={{0,1},{1,2},{2,3},{4,5},{5,6},{6,7},{8,9},{9,10},{10,11},{12,13},{... | collective-permute-start | bytes 122888 | tf_op jit(solution)/shard_map/ppermute | solution.py:17
  143.8 5.2 %collective-permute-start.21 = (f32[80,128]{1,0:T(8,128)S(1)}, f32[80,128]{1,0:T(8,128)S(1)}, u32[]{:S(2)}, u32[]{:S(2)}) collective-permute-start(f32[80,128]{1,0:T(8,128)S(1)} %get-tuple-element.13), channel_id=1, source_target_pairs={{4,0},{8,4},{12,8},{16,12},{20,16},{24,20},{28,24},{32,28},{36,32}... | collective-permute-start | bytes 122888 | tf_op jit(solution)/shard_map/ppermute | solution.py:19
  149.1 1.6 collective-permute-done.21
  150.9 1.0 gather_fusion.35
  155.7 1.2 fusion.12
  160.0 1.9 %collective-permute-start.24 = (f32[80,128]{1,0:T(8,128)S(1)}, f32[80,128]{1,0:T(8,128)S(1)}, u32[]{:S(2)}, u32[]{:S(2)}) collective-permute-start(f32[80,128]{1,0:T(8,128)S(1)} %get-tuple-element.10), channel_id=1, source_target_pairs={{0,4},{4,8},{8,12},{12,16},{16,20},{20,24},{24,28},{28,32},{32,36}... | collective-permute-start | bytes 122888 | tf_op jit(solution)/shard_map/ppermute | solution.py:17
  161.9 1.3 collective-permute-start.27
  163.2 4.5 %collective-permute-start.26 = (f32[80,128]{1,0:T(8,128)S(1)}, f32[80,128]{1,0:T(8,128)S(1)}, u32[]{:S(2)}, u32[]{:S(2)}) collective-permute-start(f32[80,128]{1,0:T(8,128)S(1)} %get-tuple-element.8), channel_id=1, source_target_pairs={{0,1},{1,2},{2,3},{4,5},{5,6},{6,7},{8,9},{9,10},{10,11},{12,13},{... | collective-permute-start | bytes 122888 | tf_op jit(solution)/shard_map/ppermute | solution.py:17
  167.8 5.2 %collective-permute-start.25 = (f32[80,128]{1,0:T(8,128)S(1)}, f32[80,128]{1,0:T(8,128)S(1)}, u32[]{:S(2)}, u32[]{:S(2)}) collective-permute-start(f32[80,128]{1,0:T(8,128)S(1)} %get-tuple-element.9), channel_id=1, source_target_pairs={{4,0},{8,4},{12,8},{16,12},{20,16},{24,20},{28,24},{32,28},{36,32}... | collective-permute-start | bytes 122888 | tf_op jit(solution)/shard_map/ppermute | solution.py:19
  173.0 1.6 collective-permute-done.25
  174.9 1.0 gather_fusion.41
  177.0 1.0 gather_fusion.39
  179.6 1.9 %fusion.9 = f32[80,512]{1,0:T(8,128)} fusion(f32[80,512]{1,0:T(8,128)S(1)} %fusion.12, f32[512,80]{0,1:T(8,128)S(1)} %fusion.134, f32[80,320]{1,0:T(8,128)S(1)} %copy-done, f32[80,512]{0,1:T(8,128)S(1)} %select_bitcast_fusion, f32[80,512]{0,1:T(8,128)S(1)} %select_bitcast_fusion.1, f32[80,512]{0,1:T(8,128)S(1)} %select_bitcast_fusion.2, ...), kind=kOutput, calls=%fused_computation.58 | convolution fusion | flops 157941760 | bytes 1251328 | tf_op jit(solution)/shard_map/dot_general | solution.py:74
  (212 shorter events, 36.5 us)
Async XLA Ops:
  0.0 35.3 %copy-start = (f32[80,320]{1,0:T(8,128)S(1)}, f32[80,320]{1,0:T(8,128)}, u32[]{:S(2)}) copy-start(f32[80,320]{1,0:T(8,128)} %param.19) | copy-start | bytes 307204
  0.0 2.2 %copy-start.1 = (f32[80,80]{1,0:T(8,128)S(1)}, f32[80,80]{1,0:T(8,128)}, u32[]{:S(2)}) copy-start(f32[80,80]{1,0:T(8,128)} %param.17) | copy-start | bytes 76804
  3.4 0.9 copy-start.3
  5.6 24.7 %collective-permute-start.3 = (f32[80,128]{1,0:T(8,128)S(1)}, f32[80,128]{1,0:T(8,128)S(1)}, u32[]{:S(2)}, u32[]{:S(2)}) collective-permute-start(f32[80,128]{1,0:T(8,128)S(1)} %get-tuple-element.31), channel_id=1, source_target_pairs={{1,0},{2,1},{3,2},{5,4},{6,5},{7,6},{9,8},{10,9},{11,10},{13,12},{... | collective-permute-start | bytes 122888 | tf_op jit(solution)/shard_map/ppermute | solution.py:19
  6.9 23.4 %collective-permute-start.2 = (f32[80,128]{1,0:T(8,128)S(1)}, f32[80,128]{1,0:T(8,128)S(1)}, u32[]{:S(2)}, u32[]{:S(2)}) collective-permute-start(f32[80,128]{1,0:T(8,128)S(1)} %get-tuple-element.32), channel_id=1, source_target_pairs={{0,1},{1,2},{2,3},{4,5},{5,6},{6,7},{8,9},{9,10},{10,11},{12,13},{... | collective-permute-start | bytes 122888 | tf_op jit(solution)/shard_map/ppermute | solution.py:17
  12.3 12.4 %copy-start.5 = (s32[4,512]{1,0:T(4,128)S(1)}, s32[4,512]{1,0:T(4,128)}, u32[]{:S(2)}) copy-start(s32[4,512]{1,0:T(4,128)} %param.15) | copy-start | bytes 24580
  12.4 12.5 %copy-start.2 = (f32[80,80]{1,0:T(8,128)S(1)}, f32[80,80]{1,0:T(8,128)}, u32[]{:S(2)}) copy-start(f32[80,80]{1,0:T(8,128)} %param.18) | copy-start | bytes 76804
  12.4 17.9 %collective-permute-start.1 = (f32[80,128]{1,0:T(8,128)S(1)}, f32[80,128]{1,0:T(8,128)S(1)}, u32[]{:S(2)}, u32[]{:S(2)}) collective-permute-start(f32[80,128]{1,0:T(8,128)S(1)} %get-tuple-element.33), channel_id=1, source_target_pairs={{4,0},{8,4},{12,8},{16,12},{20,16},{24,20},{28,24},{32,28},{36,32}... | collective-permute-start | bytes 122888 | tf_op jit(solution)/shard_map/ppermute | solution.py:19
  22.8 7.4 %collective-permute-start = (f32[80,128]{1,0:T(8,128)S(1)}, f32[80,128]{1,0:T(8,128)S(1)}, u32[]{:S(2)}, u32[]{:S(2)}) collective-permute-start(f32[80,128]{1,0:T(8,128)S(1)} %get-tuple-element.34), channel_id=1, source_target_pairs={{0,4},{4,8},{8,12},{12,16},{16,20},{20,24},{24,28},{28,32},{32,36}... | collective-permute-start | bytes 122888 | tf_op jit(solution)/shard_map/ppermute | solution.py:17
  35.2 0.7 copy-start.4
  40.1 13.0 %collective-permute-start.4 = (f32[80,128]{1,0:T(8,128)S(1)}, f32[80,128]{1,0:T(8,128)S(1)}, u32[]{:S(2)}, u32[]{:S(2)}) collective-permute-start(f32[80,128]{1,0:T(8,128)S(1)} %get-tuple-element.30), channel_id=1, source_target_pairs={{0,4},{4,8},{8,12},{12,16},{16,20},{20,24},{24,28},{28,32},{32,36}... | collective-permute-start | bytes 122888 | tf_op jit(solution)/shard_map/ppermute | solution.py:17
  42.1 12.7 %collective-permute-start.7 = (f32[80,128]{1,0:T(8,128)S(1)}, f32[80,128]{1,0:T(8,128)S(1)}, u32[]{:S(2)}, u32[]{:S(2)}) collective-permute-start(f32[80,128]{1,0:T(8,128)S(1)} %get-tuple-element.27), channel_id=1, source_target_pairs={{1,0},{2,1},{3,2},{5,4},{6,5},{7,6},{9,8},{10,9},{11,10},{13,12},{... | collective-permute-start | bytes 122888 | tf_op jit(solution)/shard_map/ppermute | solution.py:19
  43.4 11.4 %collective-permute-start.6 = (f32[80,128]{1,0:T(8,128)S(1)}, f32[80,128]{1,0:T(8,128)S(1)}, u32[]{:S(2)}, u32[]{:S(2)}) collective-permute-start(f32[80,128]{1,0:T(8,128)S(1)} %get-tuple-element.28), channel_id=1, source_target_pairs={{0,1},{1,2},{2,3},{4,5},{5,6},{6,7},{8,9},{9,10},{10,11},{12,13},{... | collective-permute-start | bytes 122888 | tf_op jit(solution)/shard_map/ppermute | solution.py:17
  47.9 6.9 %collective-permute-start.5 = (f32[80,128]{1,0:T(8,128)S(1)}, f32[80,128]{1,0:T(8,128)S(1)}, u32[]{:S(2)}, u32[]{:S(2)}) collective-permute-start(f32[80,128]{1,0:T(8,128)S(1)} %get-tuple-element.29), channel_id=1, source_target_pairs={{4,0},{8,4},{12,8},{16,12},{20,16},{24,20},{28,24},{32,28},{36,32}... | collective-permute-start | bytes 122888 | tf_op jit(solution)/shard_map/ppermute | solution.py:19
  64.1 13.2 %collective-permute-start.8 = (f32[80,128]{1,0:T(8,128)S(1)}, f32[80,128]{1,0:T(8,128)S(1)}, u32[]{:S(2)}, u32[]{:S(2)}) collective-permute-start(f32[80,128]{1,0:T(8,128)S(1)} %get-tuple-element.26), channel_id=1, source_target_pairs={{0,4},{4,8},{8,12},{12,16},{16,20},{20,24},{24,28},{28,32},{32,36}... | collective-permute-start | bytes 122888 | tf_op jit(solution)/shard_map/ppermute | solution.py:17
  66.0 12.8 %collective-permute-start.11 = (f32[80,128]{1,0:T(8,128)S(1)}, f32[80,128]{1,0:T(8,128)S(1)}, u32[]{:S(2)}, u32[]{:S(2)}) collective-permute-start(f32[80,128]{1,0:T(8,128)S(1)} %get-tuple-element.23), channel_id=1, source_target_pairs={{1,0},{2,1},{3,2},{5,4},{6,5},{7,6},{9,8},{10,9},{11,10},{13,12},{... | collective-permute-start | bytes 122888 | tf_op jit(solution)/shard_map/ppermute | solution.py:19
  67.3 11.4 %collective-permute-start.10 = (f32[80,128]{1,0:T(8,128)S(1)}, f32[80,128]{1,0:T(8,128)S(1)}, u32[]{:S(2)}, u32[]{:S(2)}) collective-permute-start(f32[80,128]{1,0:T(8,128)S(1)} %get-tuple-element.24), channel_id=1, source_target_pairs={{0,1},{1,2},{2,3},{4,5},{5,6},{6,7},{8,9},{9,10},{10,11},{12,13},{... | collective-permute-start | bytes 122888 | tf_op jit(solution)/shard_map/ppermute | solution.py:17
  71.9 6.9 %collective-permute-start.9 = (f32[80,128]{1,0:T(8,128)S(1)}, f32[80,128]{1,0:T(8,128)S(1)}, u32[]{:S(2)}, u32[]{:S(2)}) collective-permute-start(f32[80,128]{1,0:T(8,128)S(1)} %get-tuple-element.25), channel_id=1, source_target_pairs={{4,0},{8,4},{12,8},{16,12},{20,16},{24,20},{28,24},{32,28},{36,32}... | collective-permute-start | bytes 122888 | tf_op jit(solution)/shard_map/ppermute | solution.py:19
  88.1 13.0 %collective-permute-start.12 = (f32[80,128]{1,0:T(8,128)S(1)}, f32[80,128]{1,0:T(8,128)S(1)}, u32[]{:S(2)}, u32[]{:S(2)}) collective-permute-start(f32[80,128]{1,0:T(8,128)S(1)} %get-tuple-element.22), channel_id=1, source_target_pairs={{0,4},{4,8},{8,12},{12,16},{16,20},{20,24},{24,28},{28,32},{32,36}... | collective-permute-start | bytes 122888 | tf_op jit(solution)/shard_map/ppermute | solution.py:17
  90.0 12.7 %collective-permute-start.15 = (f32[80,128]{1,0:T(8,128)S(1)}, f32[80,128]{1,0:T(8,128)S(1)}, u32[]{:S(2)}, u32[]{:S(2)}) collective-permute-start(f32[80,128]{1,0:T(8,128)S(1)} %get-tuple-element.19), channel_id=1, source_target_pairs={{1,0},{2,1},{3,2},{5,4},{6,5},{7,6},{9,8},{10,9},{11,10},{13,12},{... | collective-permute-start | bytes 122888 | tf_op jit(solution)/shard_map/ppermute | solution.py:19
  91.3 11.4 %collective-permute-start.14 = (f32[80,128]{1,0:T(8,128)S(1)}, f32[80,128]{1,0:T(8,128)S(1)}, u32[]{:S(2)}, u32[]{:S(2)}) collective-permute-start(f32[80,128]{1,0:T(8,128)S(1)} %get-tuple-element.20), channel_id=1, source_target_pairs={{0,1},{1,2},{2,3},{4,5},{5,6},{6,7},{8,9},{9,10},{10,11},{12,13},{... | collective-permute-start | bytes 122888 | tf_op jit(solution)/shard_map/ppermute | solution.py:17
  95.9 6.9 %collective-permute-start.13 = (f32[80,128]{1,0:T(8,128)S(1)}, f32[80,128]{1,0:T(8,128)S(1)}, u32[]{:S(2)}, u32[]{:S(2)}) collective-permute-start(f32[80,128]{1,0:T(8,128)S(1)} %get-tuple-element.21), channel_id=1, source_target_pairs={{4,0},{8,4},{12,8},{16,12},{20,16},{24,20},{28,24},{32,28},{36,32}... | collective-permute-start | bytes 122888 | tf_op jit(solution)/shard_map/ppermute | solution.py:19
  112.0 13.0 %collective-permute-start.16 = (f32[80,128]{1,0:T(8,128)S(1)}, f32[80,128]{1,0:T(8,128)S(1)}, u32[]{:S(2)}, u32[]{:S(2)}) collective-permute-start(f32[80,128]{1,0:T(8,128)S(1)} %get-tuple-element.18), channel_id=1, source_target_pairs={{0,4},{4,8},{8,12},{12,16},{16,20},{20,24},{24,28},{28,32},{32,36}... | collective-permute-start | bytes 122888 | tf_op jit(solution)/shard_map/ppermute | solution.py:17
  114.0 12.7 %collective-permute-start.19 = (f32[80,128]{1,0:T(8,128)S(1)}, f32[80,128]{1,0:T(8,128)S(1)}, u32[]{:S(2)}, u32[]{:S(2)}) collective-permute-start(f32[80,128]{1,0:T(8,128)S(1)} %get-tuple-element.15), channel_id=1, source_target_pairs={{1,0},{2,1},{3,2},{5,4},{6,5},{7,6},{9,8},{10,9},{11,10},{13,12},{... | collective-permute-start | bytes 122888 | tf_op jit(solution)/shard_map/ppermute | solution.py:19
  115.3 11.4 %collective-permute-start.18 = (f32[80,128]{1,0:T(8,128)S(1)}, f32[80,128]{1,0:T(8,128)S(1)}, u32[]{:S(2)}, u32[]{:S(2)}) collective-permute-start(f32[80,128]{1,0:T(8,128)S(1)} %get-tuple-element.16), channel_id=1, source_target_pairs={{0,1},{1,2},{2,3},{4,5},{5,6},{6,7},{8,9},{9,10},{10,11},{12,13},{... | collective-permute-start | bytes 122888 | tf_op jit(solution)/shard_map/ppermute | solution.py:17
  119.8 6.9 %collective-permute-start.17 = (f32[80,128]{1,0:T(8,128)S(1)}, f32[80,128]{1,0:T(8,128)S(1)}, u32[]{:S(2)}, u32[]{:S(2)}) collective-permute-start(f32[80,128]{1,0:T(8,128)S(1)} %get-tuple-element.17), channel_id=1, source_target_pairs={{4,0},{8,4},{12,8},{16,12},{20,16},{24,20},{28,24},{32,28},{36,32}... | collective-permute-start | bytes 122888 | tf_op jit(solution)/shard_map/ppermute | solution.py:19
  136.0 13.0 %collective-permute-start.20 = (f32[80,128]{1,0:T(8,128)S(1)}, f32[80,128]{1,0:T(8,128)S(1)}, u32[]{:S(2)}, u32[]{:S(2)}) collective-permute-start(f32[80,128]{1,0:T(8,128)S(1)} %get-tuple-element.14), channel_id=1, source_target_pairs={{0,4},{4,8},{8,12},{12,16},{16,20},{20,24},{24,28},{28,32},{32,36}... | collective-permute-start | bytes 122888 | tf_op jit(solution)/shard_map/ppermute | solution.py:17
  137.9 12.8 %collective-permute-start.23 = (f32[80,128]{1,0:T(8,128)S(1)}, f32[80,128]{1,0:T(8,128)S(1)}, u32[]{:S(2)}, u32[]{:S(2)}) collective-permute-start(f32[80,128]{1,0:T(8,128)S(1)} %get-tuple-element.11), channel_id=1, source_target_pairs={{1,0},{2,1},{3,2},{5,4},{6,5},{7,6},{9,8},{10,9},{11,10},{13,12},{... | collective-permute-start | bytes 122888 | tf_op jit(solution)/shard_map/ppermute | solution.py:19
  139.2 11.5 %collective-permute-start.22 = (f32[80,128]{1,0:T(8,128)S(1)}, f32[80,128]{1,0:T(8,128)S(1)}, u32[]{:S(2)}, u32[]{:S(2)}) collective-permute-start(f32[80,128]{1,0:T(8,128)S(1)} %get-tuple-element.12), channel_id=1, source_target_pairs={{0,1},{1,2},{2,3},{4,5},{5,6},{6,7},{8,9},{9,10},{10,11},{12,13},{... | collective-permute-start | bytes 122888 | tf_op jit(solution)/shard_map/ppermute | solution.py:17
  143.8 6.9 %collective-permute-start.21 = (f32[80,128]{1,0:T(8,128)S(1)}, f32[80,128]{1,0:T(8,128)S(1)}, u32[]{:S(2)}, u32[]{:S(2)}) collective-permute-start(f32[80,128]{1,0:T(8,128)S(1)} %get-tuple-element.13), channel_id=1, source_target_pairs={{4,0},{8,4},{12,8},{16,12},{20,16},{24,20},{28,24},{32,28},{36,32}... | collective-permute-start | bytes 122888 | tf_op jit(solution)/shard_map/ppermute | solution.py:19
  160.0 13.0 %collective-permute-start.24 = (f32[80,128]{1,0:T(8,128)S(1)}, f32[80,128]{1,0:T(8,128)S(1)}, u32[]{:S(2)}, u32[]{:S(2)}) collective-permute-start(f32[80,128]{1,0:T(8,128)S(1)} %get-tuple-element.10), channel_id=1, source_target_pairs={{0,4},{4,8},{8,12},{12,16},{16,20},{20,24},{24,28},{28,32},{32,36}... | collective-permute-start | bytes 122888 | tf_op jit(solution)/shard_map/ppermute | solution.py:17
  161.9 12.7 %collective-permute-start.27 = (f32[80,128]{1,0:T(8,128)S(1)}, f32[80,128]{1,0:T(8,128)S(1)}, u32[]{:S(2)}, u32[]{:S(2)}) collective-permute-start(f32[80,128]{1,0:T(8,128)S(1)} %get-tuple-element.6), channel_id=1, source_target_pairs={{1,0},{2,1},{3,2},{5,4},{6,5},{7,6},{9,8},{10,9},{11,10},{13,12},{... | collective-permute-start | bytes 122888 | tf_op jit(solution)/shard_map/ppermute | solution.py:19
  163.2 11.4 %collective-permute-start.26 = (f32[80,128]{1,0:T(8,128)S(1)}, f32[80,128]{1,0:T(8,128)S(1)}, u32[]{:S(2)}, u32[]{:S(2)}) collective-permute-start(f32[80,128]{1,0:T(8,128)S(1)} %get-tuple-element.8), channel_id=1, source_target_pairs={{0,1},{1,2},{2,3},{4,5},{5,6},{6,7},{8,9},{9,10},{10,11},{12,13},{... | collective-permute-start | bytes 122888 | tf_op jit(solution)/shard_map/ppermute | solution.py:17
  167.8 6.9 %collective-permute-start.25 = (f32[80,128]{1,0:T(8,128)S(1)}, f32[80,128]{1,0:T(8,128)S(1)}, u32[]{:S(2)}, u32[]{:S(2)}) collective-permute-start(f32[80,128]{1,0:T(8,128)S(1)} %get-tuple-element.9), channel_id=1, source_target_pairs={{4,0},{8,4},{12,8},{16,12},{20,16},{24,20},{28,24},{32,28},{36,32}... | collective-permute-start | bytes 122888 | tf_op jit(solution)/shard_map/ppermute | solution.py:19
where the time goes:
time: 183 us; the launch traced here: 182 us
  starting transfers between devices  96.2 us (53%)
  local copies, waits for them, and re-layouts  44.8 us (24%)
  matrix products  18.7 us (10%)
  waiting for transfers between devices  14.7 us (8%)
  other arithmetic  5.36 us (3%)
    ppermute x14, starting transfers between devices, with_halo(): lax.ppermute(head, axis, [((i + 1) % count, i) for i in range(ends)])  50.9 us
    ppermute x14, starting transfers between devices, with_halo(): lax.ppermute(tail, axis, [(i, (i + 1) % count) for i in range(ends)])  45.3 us
    gather x28, local copies, waits for them, and re-layouts, shards(): jnp.take(extended, face_links[face_id], axis=1)  29 us
    ppermute x14, waiting for transfers between devices, with_halo(): lax.ppermute(head, axis, [((i + 1) % count, i) for i in range(ends)])  9.61 us
    dot_general x7, matrix products, shards(): coupled = jnp.dot(w_neighbour, stacked, precision=lax.Precision.HIGHEST)  9.39 us
    dot_general x21, matrix products, predict(): jnp.dot(k_matrix, current, precision=lax.Precision.HIGHEST)  7.23 us
    gather x14, local copies, waits for them, and re-layouts, shards(): jnp.take(predicted, halo_list[1], axis=1)  5.71 us
    gather x14, local copies, waits for them, and re-layouts, shards(): jnp.take(predicted, halo_list[0], axis=1)  5.67 us
  transfers between devices with their start and end apart: 28, of which 7 were waited for; matrix products, arithmetic and copies ran while one was open for 1% of the time, Pallas kernels for 0%

commit v1 on v0

v1 whole, which is shorter than its diff:
```python
import functools

import jax
import jax.numpy as jnp
from jax import lax
from jax.experimental import pallas as pl
from jax.experimental.pallas import tpu as pltpu
from jax.sharding import PartitionSpec as P

MESH = pl.DeviceIdType.MESH
F32 = jnp.float32
BF16 = jnp.bfloat16

TIME_STEP = 0.125
CAP = 48
LANES = 128
LEVELS = (2, 1, 0, 0, 1, 0, 0)


def dot(a, b):
    return lax.dot_general(a, b, (((1,), (0,)), ((), ())), preferred_element_type=F32)


def dot_nt(a, b):
    return lax.dot_general(a, b, (((1,), (1,)), ((), ())), preferred_element_type=F32)


def dot_full(a, b):
    return lax.dot_general(
        a, b, (((1,), (0,)), ((), ())), precision=lax.Precision.HIGHEST, preferred_element_type=F32
    )


def split2(x):
    hi = x.astype(BF16)
    return hi, (x - hi.astype(F32)).astype(BF16)


def split3(x):
    hi = x.astype(BF16)
    rest = x - hi.astype(F32)
    mid = rest.astype(BF16)
    return hi, mid, (rest - mid.astype(F32)).astype(BF16)


def left_pieces(x):
    hi, lo = split2(x)
    return jnp.concatenate([hi, lo, hi], axis=1)


def ones_where(mask):
    return jnp.where(mask, 1.0, 0.0).astype(BF16)


def kernel(
    n_slab,
    n_sub,
    adjoint_ref,
    scale_ref,
    cluster_ref,
    links_ref,
    list_ref,
    k_ref,
    self_ref,
    neighbour_ref,
    out_ref,
    x_ref,
    h_ref,
    q_ref,
    pt_ref,
    state_ref,
    factor_ref,
    linkb_ref,
    own_m_ref,
    halo_m_ref,
    g_own_ref,
    g_halo_ref,
    kk_ref,
    nn_ref,
    pad_ref,
    send_ref,
    recv_ref,
    id_send_ref,
    id_recv_ref,
    send_sem,
    recv_sem,
    id_send_sem,
    id_recv_sem,
):
    dofs, elems = adjoint_ref.shape
    side = elems // 4
    per = 4 * CAP
    slots = 3 * per

    i = lax.axis_index("slab")
    j = lax.axis_index("sub")
    low = ((i - 1, j), (i, j - 1))
    has_low = (i > 0, j > 0)
    high = ((i + 1, j), (i, j + 1))
    has_high = (i < n_slab - 1, j < n_sub - 1)
    target = (low[0], high[0], low[1], high[1])
    has_target = (has_low[0], has_high[0], has_low[1], has_high[1])
    has_source = (has_high[0], has_low[0], has_high[1], has_low[1])
    link_base = (elems + side, elems, elems + 3 * side, elems + 2 * side)

    barrier = pltpu.get_barrier_semaphore()
    for h in range(4):

        @pl.when(has_target[h])
        def _(h=h):
            pl.semaphore_signal(barrier, inc=1, device_id=target[h], device_id_type=MESH)

    def wave(k, h):
        return pltpu.make_async_remote_copy(
            src_ref=send_ref.at[k, pl.ds(h * CAP, CAP)],
            dst_ref=recv_ref.at[k, pl.ds(h * CAP, CAP)],
            send_sem=send_sem.at[k, h],
            recv_sem=recv_sem.at[k, h],
            device_id=target[h],
            device_id_type=MESH,
        )

    def id_wave(h):
        return pltpu.make_async_remote_copy(
            src_ref=id_send_ref,
            dst_ref=id_recv_ref.at[h],
            send_sem=id_send_sem.at[h],
            recv_sem=id_recv_sem.at[h],
            device_id=target[h],
            device_id_type=MESH,
        )

    def each_target(do):
        for h in range(4):

            @pl.when(has_target[h])
            def _(h=h):
                do(h)

    def each_source(do):
        for h in range(4):

            @pl.when(has_source[h])
            def _(h=h):
                do(h)

    listed = jnp.concatenate([list_ref[0:1, :], list_ref[1:2, :]], axis=1)
    h_ref[...] = ones_where(lax.broadcasted_iota(jnp.int32, (elems, elems), 0) == listed)

    cluster8 = jnp.broadcast_to(cluster_ref[...].astype(F32), (16, elems)).astype(BF16)
    cluster_p = dot(cluster8, h_ref[...])
    level_row = lax.broadcasted_iota(jnp.int32, (16, elems), 0).astype(F32)
    is_level = cluster_p == level_row
    before_from = lax.broadcasted_iota(jnp.int32, (elems, elems), 0)
    before_to = lax.broadcasted_iota(jnp.int32, (elems, elems), 1)
    before = ones_where((before_from < before_to) & (before_from // side == before_to // side))
    ranks = dot(ones_where(is_level), before)
    rank = jnp.sum(jnp.where(is_level, ranks, 0.0), axis=0, keepdims=True)
    position = lax.broadcasted_iota(jnp.int32, (1, elems), 1)
    slot = (cluster_p[0:1, :] * per + rank).astype(jnp.int32) + position // side * CAP
    q_ref[...] = ones_where(lax.broadcasted_iota(jnp.int32, (slots, elems), 0) == slot)

    side_of = position // side
    base = jnp.where(
        side_of == 0,
        link_base[0],
        jnp.where(side_of == 1, link_base[1], jnp.where(side_of == 2, link_base[2], link_base[3])),
    )
    own_plus = listed + 1
    far_plus = base + (position - side_of * side) + 1
    id_rows = jnp.concatenate(
        [
            (own_plus // 32 * 32).astype(F32),
            (own_plus % 32).astype(F32),
            (far_plus // 32 * 32).astype(F32),
            (far_plus % 32).astype(F32),
            jnp.zeros((12, elems), F32),
        ],
        axis=0,
    ).astype(BF16)
    own_ids = []
    for c in range(3):
        ids = dot_nt(id_rows, q_ref[c * per : (c + 1) * per, :])
        own = ids[0:1, :] + ids[1:2, :] - 1.0
        own_ids.append(jnp.concatenate([own, own], axis=1))
        far = ids[2:3, :] + ids[3:4, :] - 1.0
        id_send_ref[c : c + 1, :] = jnp.concatenate([far, far], axis=1)

    for h in range(4):

        @pl.when(jnp.logical_not(has_source[h]))
        def _(h=h):
            recv_ref[:, h * CAP : (h + 1) * CAP, :] = jnp.zeros((len(LEVELS), CAP, LANES), F32)
            id_recv_ref[h] = jnp.full(id_recv_ref.shape[1:], -1.0, F32)

    pl.semaphore_wait(barrier, sum(has.astype(jnp.int32) for has in has_target))
    each_target(lambda h: id_wave(h).start())

    x_ref[...] = jnp.zeros_like(x_ref)
    x_ref[0:dofs, :] = adjoint_ref[...]
    x_ref[dofs : dofs + 1, :] = scale_ref[...]
    x_ref[dofs + 1 : dofs + 5, :] = links_ref[...].astype(F32)
    moved = dot(jnp.concatenate(split3(x_ref[...]), axis=0), h_ref[...])
    moved = moved[0:LANES] + moved[LANES : 2 * LANES] + moved[2 * LANES :]
    moved3 = jnp.concatenate(split3(moved), axis=0)
    for c in (2, 1, 0):
        rows = slice(c * per, (c + 1) * per)
        placed = dot_nt(q_ref[rows, :], moved3)
        placed = placed[:, 0:LANES] + placed[:, LANES : 2 * LANES] + placed[:, 2 * LANES :]
        lane = lax.broadcasted_iota(jnp.int32, (per, LANES), 1)
        state_ref[rows, :] = jnp.where(lane < dofs, placed, 0.0)
        factor_ref[rows, :] = jnp.broadcast_to(placed[:, dofs : dofs + 1], (per, LANES))
        faces = [
            jnp.broadcast_to(placed[:, dofs + 1 + f : dofs + 2 + f], (per, LANES)) for f in range(4)
        ]
        for pair in range(2):
            first, second = faces[2 * pair], faces[2 * pair + 1]
            linkb_ref[3 * pair, rows, :] = first
            linkb_ref[3 * pair + 1, rows, :] = jnp.where(lane < LANES // 2, first, second)
            linkb_ref[3 * pair + 2, rows, :] = second

    pad_ref[...] = jnp.zeros_like(pad_ref)
    kk_ref[...] = jnp.zeros_like(kk_ref)
    pad_ref[0, 0:dofs, 0:dofs] = k_ref[...]
    pad_ref[1, 0:dofs, 0:dofs] = self_ref[...]
    for f in range(4):
        pad_ref[2 + f, 0:dofs, 0:dofs] = neighbour_ref[:, f * dofs : (f + 1) * dofs]

    def put(ref, at, matrix):
        hi, lo = split2(matrix)
        cols = slice(at * LANES, (at + 1) * LANES)
        ref[0:LANES, cols] = hi
        ref[LANES : 2 * LANES, cols] = hi
        ref[2 * LANES :, cols] = lo

    k1 = pad_ref[0].T
    k2 = dot_full(k1, k1)
    k3 = dot_full(k2, k1)
    for at, matrix in enumerate((k1, k2, k3)):
        put(kk_ref, at, matrix)
    for f in range(4):
        put(nn_ref, f, pad_ref[2 + f].T)
    put(nn_ref, 4, pad_ref[1].T)

    def step_size(c):
        return TIME_STEP * 2.0**c

    def rows_of(c):
        return slice(c * per, (c + 1) * per)

    def predict_and_send(k):
        c = LEVELS[k]
        v = state_ref[rows_of(c), :]
        terms = dot(left_pieces(v), kk_ref[...])
        a = step_size(c) * factor_ref[rows_of(c), :]
        w = (
            v
            + a * (1.0 / 2.0) * terms[:, 0:LANES]
            + a * a * (1.0 / 6.0) * terms[:, LANES : 2 * LANES]
            + a * a * a * (1.0 / 24.0) * terms[:, 2 * LANES :]
        )
        send_ref[k] = w
        each_target(lambda h: wave(k, h).start())

    def build(m_ref, c, ids):
        for block in range(6):
            row = ids[:, block % 3 * LANES : (block % 3 + 1) * LANES]
            m_ref[c, :, block * LANES : (block + 1) * LANES] = ones_where(linkb_ref[block] == row)

    def spread(g_ref, product):
        for f in range(4):
            hi, lo = split2(product[:, f * LANES : (f + 1) * LANES])
            g_ref[f * per : (f + 1) * per, 0:LANES] = hi
            g_ref[f * per : (f + 1) * per, LANES : 2 * LANES] = lo

    def gather(m_ref, g_ref, c, d):
        both = dot(m_ref[c, rows_of(d), :], g_ref[...])
        return both[:, 0:LANES] + both[:, LANES:]

    def add(c, d, change):
        a = step_size(c) * factor_ref[rows_of(d), :]
        state_ref[rows_of(d), :] += a * change

    seen = set()
    predict_and_send(0)
    each_source(lambda h: id_wave(h).wait_recv())
    for k, c in enumerate(LEVELS):
        if c not in seen:
            build(own_m_ref, c, own_ids[c])
        product = dot(left_pieces(send_ref[k]), nn_ref[...])
        spread(g_own_ref, product)
        for d in range(3):
            change = gather(own_m_ref, g_own_ref, c, d)
            if d == c:
                change = change + product[:, 4 * LANES :]
            add(c, d, change)
        if c not in seen:
            seen.add(c)
            lane = lax.broadcasted_iota(jnp.int32, (1, 2 * per), 1) % per
            ids = jnp.where(
                lane < CAP,
                id_recv_ref[0, c : c + 1, :],
                jnp.where(
                    lane < 2 * CAP,
                    id_recv_ref[1, c : c + 1, :],
                    jnp.where(lane < 3 * CAP, id_recv_ref[2, c : c + 1, :], id_recv_ref[3, c : c + 1, :]),
                ),
            )
            build(halo_m_ref, c, ids)
        if k == 0:
            pt_ref[...] = dot_nt(h_ref[...], q_ref[...]).astype(BF16)
        each_source(lambda h, k=k: wave(k, h).wait_recv())
        product = dot(left_pieces(recv_ref[k]), nn_ref[:, 0 : 4 * LANES])
        spread(g_halo_ref, product)
        order = [0, 1, 2]
        if k + 1 < len(LEVELS):
            order = [LEVELS[k + 1]] + [d for d in order if d != LEVELS[k + 1]]
        for at, d in enumerate(order):
            add(c, d, gather(halo_m_ref, g_halo_ref, c, d))
            if at == 0 and k + 1 < len(LEVELS):
                predict_and_send(k + 1)

    final = dot(pt_ref[...], jnp.concatenate(split3(state_ref[...]), axis=1))
    final = final[:, 0:LANES] + final[:, LANES : 2 * LANES] + final[:, 2 * LANES :]
    out_ref[...] = final.T[0:dofs, :]

    each_target(lambda h: id_wave(h).wait_send())
    for k in range(len(LEVELS)):
        each_target(lambda h, k=k: wave(k, h).wait_send())


def shards(n_slab, n_sub, adjoint, elem_scale, cluster, face_links, halo_list, k_matrix, w_self, w_neighbour):
    dofs, elems = adjoint.shape
    per = 4 * CAP
    slots = 3 * per
    count = len(LEVELS)
    vmem = pl.BlockSpec(memory_space=pltpu.VMEM)
    return pl.pallas_call(
        functools.partial(kernel, n_slab, n_sub),
        out_shape=jax.ShapeDtypeStruct((dofs, elems), F32),
        in_specs=[vmem] * 8,
        out_specs=vmem,
        scratch_shapes=[
            pltpu.VMEM((LANES, elems), F32),
            pltpu.VMEM((elems, elems), BF16),
            pltpu.VMEM((slots, elems), BF16),
            pltpu.VMEM((elems, slots), BF16),
            pltpu.VMEM((slots, LANES), F32),
            pltpu.VMEM((slots, LANES), F32),
            pltpu.VMEM((6, slots, LANES), F32),
            pltpu.VMEM((3, slots, 4 * per), BF16),
            pltpu.VMEM((3, slots, 4 * per), BF16),
            pltpu.VMEM((4 * per, 2 * LANES), BF16),
            pltpu.VMEM((4 * per, 2 * LANES), BF16),
            pltpu.VMEM((3 * LANES, 3 * LANES), BF16),
            pltpu.VMEM((3 * LANES, 5 * LANES), BF16),
            pltpu.VMEM((6, LANES, LANES), F32),
            pltpu.VMEM((count, per, LANES), F32),
            pltpu.VMEM((count, per, LANES), F32),
            pltpu.VMEM((8, 2 * per), F32),
            pltpu.VMEM((4, 8, 2 * per), F32),
            pltpu.SemaphoreType.DMA((count, 4)),
            pltpu.SemaphoreType.DMA((count, 4)),
            pltpu.SemaphoreType.DMA((4,)),
            pltpu.SemaphoreType.DMA((4,)),
        ],
        compiler_params=pltpu.CompilerParams(
            collective_id=0, has_side_effects=True, vmem_limit_bytes=40 * 1024 * 1024
        ),
    )(
        adjoint,
        elem_scale.reshape(1, elems),
        cluster.reshape(1, elems),
        face_links,
        halo_list,
        k_matrix,
        w_self,
        w_neighbour,
    )


def solution(mesh):
    placed = (
        P(None, ("slab", "sub")),
        P(("slab", "sub")),
        P(("slab", "sub")),
        P(None, ("slab", "sub")),
        P(None, ("slab", "sub")),
        P(),
        P(),
        P(),
    )
    return jax.shard_map(
        functools.partial(shards, mesh.shape["slab"], mesh.shape["sub"]),
        mesh=mesh,
        in_specs=placed,
        out_specs=P(None, ("slab", "sub")),
        check_vma=False,
    )
```

time: 183 us -> 49.1 us (0.27)
  starting transfers between devices: 96.2 us -> 0 us
  Pallas kernels: 0 us -> 41.9 us
  local copies, waits for them, and re-layouts: 44.8 us -> 6.78 us
  matrix products: 18.7 us -> 0 us
  waiting for transfers between devices: 14.7 us -> 0 us
  other arithmetic: 5.36 us -> 0 us
    ppermute x28 -> x0, starting transfers between devices: 96.2 us -> none  [the longest x14 50.9 us: with_halo(): lax.ppermute(head, axis, [((i + 1) % count, i) for i in range(ends)])]
    pallas_call x0 -> x1, Pallas kernels: none -> 41.9 us  [shards(): pl.pallas_call(functools.partial(kernel, n_slab, n_sub), out_shape=jax.Sh...]
    gather x56 -> x0, local copies, waits for them, and re-layouts: 40.4 us -> none  [the longest x28 29 us: shards(): jnp.take(extended, face_links[face_id], axis=1)]
    dot_general x35 -> x0, matrix products: 18.7 us -> none  [the longest x7 9.39 us: shards(): coupled = jnp.dot(w_neighbour, stacked, precision=lax.Precision.HIGHEST)]
    ppermute x28 -> x0, waiting for transfers between devices: 14.7 us -> none  [the longest x14 9.61 us: with_halo(): lax.ppermute(head, axis, [((i + 1) % count, i) for i in range(ends)])]
    unnamed x33 -> x17, local copies, waits for them, and re-layouts: 1.26 us -> 6.78 us
    select_n x48 -> x0, other arithmetic: 3.92 us -> none  [the longest x32 3.77 us: shards(): jnp.take(extended, face_links[face_id], axis=1)]
  transfers between devices with their start and end apart: 28 -> 0, of which waited for: 7 -> 0; matrix products, arithmetic and copies ran while one was open for 1% -> 0% of each run, Pallas kernels for 0% -> 0%
where the time goes in v1:
time: 49.1 us; the launch traced here: 48.7 us
  Pallas kernels  41.9 us (85%)
  local copies, waits for them, and re-layouts  6.78 us (14%)
    pallas_call x1, Pallas kernels, shards(): pl.pallas_call(functools.partial(kernel, n_slab, n_sub), out_shape=jax.Sh...  41.9 us
    unnamed x17, local copies, waits for them, and re-layouts  6.78 us

profile of v1, /device:TPU:24, one launch (start us, length us, event | category | flops | bytes accessed | tf_op | source)
XLA Modules:
  0.0 48.7 jit_solution(16889412758393970877)
XLA Ops:
  0.0 0.0 copy-start.5
  0.0 0.7 %copy-done.5 = f32[512]{0:T(512)S(1)} copy-done((f32[512]{0:T(512)S(1)}, f32[512]{0:T(512)}, u32[]{:S(2)}) %copy-start.5) | copy-done | bytes 2072
  0.7 0.0 copy-start
  0.7 0.9 %copy-done = f32[80,512]{1,0:T(8,128)S(1)} copy-done((f32[80,512]{1,0:T(8,128)S(1)}, f32[80,512]{1,0:T(8,128)}, u32[]{:S(2)}) %copy-start) | copy-done | bytes 163864
  1.6 0.0 copy-start.1
  1.6 0.9 %copy-done.1 = f32[80,320]{1,0:T(8,128)S(1)} copy-done((f32[80,320]{1,0:T(8,128)S(1)}, f32[80,320]{1,0:T(8,128)}, u32[]{:S(2)}) %copy-start.1) | copy-done | bytes 102424
  2.5 0.0 copy-start.2
  2.5 0.8 %copy-done.2 = f32[80,80]{1,0:T(8,128)S(1)} copy-done((f32[80,80]{1,0:T(8,128)S(1)}, f32[80,80]{1,0:T(8,128)}, u32[]{:S(2)}) %copy-start.2) | copy-done | bytes 25624
  3.3 0.0 copy-start.3
  3.3 0.8 %copy-done.3 = f32[80,80]{1,0:T(8,128)S(1)} copy-done((f32[80,80]{1,0:T(8,128)S(1)}, f32[80,80]{1,0:T(8,128)}, u32[]{:S(2)}) %copy-start.3) | copy-done | bytes 25624
  4.1 0.0 copy-start.4
  4.1 0.7 %copy-done.4 = s32[4,512]{1,0:T(4,128)S(1)} copy-done((s32[4,512]{1,0:T(4,128)S(1)}, s32[4,512]{1,0:T(4,128)}, u32[]{:S(2)}) %copy-start.4) | copy-done | bytes 8216
  4.8 0.0 copy-start.6
  4.8 0.7 %copy-done.6 = s32[512]{0:T(512)S(1)} copy-done((s32[512]{0:T(512)S(1)}, s32[512]{0:T(512)}, u32[]{:S(2)}) %copy-start.6) | copy-done | bytes 2072
  5.4 0.0 copy-start.7
  5.4 0.7 %copy-done.7 = s32[2,256]{1,0:T(2,128)S(1)} copy-done((s32[2,256]{1,0:T(2,128)S(1)}, s32[2,256]{1,0:T(2,128)}, u32[]{:S(2)}) %copy-start.7) | copy-done | bytes 2072
  6.1 41.9 %shard_map.82 = f32[80,512]{1,0:T(8,128)S(1)} custom-call(f32[80,512]{1,0:T(8,128)S(1)} %copy-done, f32[1,512]{1,0:T(1,128)S(1)} %bitcast.2, s32[1,512]{1,0:T(1,128)S(1)} %bitcast.3, s32[4,512]{1,0:T(4,128)S(1)} %copy-done.4, s32[2,256]{1,0:T(2,128)S(1)} %copy-done.7, f32[80,80]{1,0:T(8,128)S(1)} %copy-done.2, f32[80,80]{1,0:T(8,128)S(1)} %copy-done.3, ...), custom_call_target="tpu_custom_call" | custom-call | tf_op jit(solution)/shard_map/pallas_call | solution.py:338
  48.0 0.7 %copy.10 = f32[80,512]{1,0:T(8,128)} copy(f32[80,512]{1,0:T(8,128)S(1)} %shard_map.82) | data formatting | bytes 327680
Async XLA Ops:
  0.0 0.7 %copy-start.5 = (f32[512]{0:T(512)S(1)}, f32[512]{0:T(512)}, u32[]{:S(2)}) copy-start(f32[512]{0:T(512)} %param.9) | copy-start | bytes 6148
  0.7 0.9 %copy-start = (f32[80,512]{1,0:T(8,128)S(1)}, f32[80,512]{1,0:T(8,128)}, u32[]{:S(2)}) copy-start(f32[80,512]{1,0:T(8,128)} %adjoint_ref.1) | copy-start | bytes 491524
  1.6 0.9 %copy-start.1 = (f32[80,320]{1,0:T(8,128)S(1)}, f32[80,320]{1,0:T(8,128)}, u32[]{:S(2)}) copy-start(f32[80,320]{1,0:T(8,128)} %neighbour_ref.1) | copy-start | bytes 307204
  2.5 0.8 %copy-start.2 = (f32[80,80]{1,0:T(8,128)S(1)}, f32[80,80]{1,0:T(8,128)}, u32[]{:S(2)}) copy-start(f32[80,80]{1,0:T(8,128)} %k_ref.1) | copy-start | bytes 76804
  3.3 0.8 %copy-start.3 = (f32[80,80]{1,0:T(8,128)S(1)}, f32[80,80]{1,0:T(8,128)}, u32[]{:S(2)}) copy-start(f32[80,80]{1,0:T(8,128)} %self_ref.1) | copy-start | bytes 76804
  4.1 0.7 %copy-start.4 = (s32[4,512]{1,0:T(4,128)S(1)}, s32[4,512]{1,0:T(4,128)}, u32[]{:S(2)}) copy-start(s32[4,512]{1,0:T(4,128)} %links_ref.1) | copy-start | bytes 24580
  4.8 0.7 %copy-start.6 = (s32[512]{0:T(512)S(1)}, s32[512]{0:T(512)}, u32[]{:S(2)}) copy-start(s32[512]{0:T(512)} %param.10) | copy-start | bytes 6148
  5.4 0.7 %copy-start.7 = (s32[2,256]{1,0:T(2,128)S(1)}, s32[2,256]{1,0:T(2,128)}, u32[]{:S(2)}) copy-start(s32[2,256]{1,0:T(2,128)} %list_ref.1) | copy-start | bytes 6148

commit v2 on v1

v2 whole, which is shorter than its diff:
```python
import functools

import jax
import jax.numpy as jnp
from jax import lax
from jax.experimental import pallas as pl
from jax.experimental.pallas import tpu as pltpu
from jax.sharding import PartitionSpec as P

MESH = pl.DeviceIdType.MESH
F32 = jnp.float32
BF16 = jnp.bfloat16

TIME_STEP = 0.125
CAP = 48
LANES = 128
LEVELS = (2, 1, 0, 0, 1, 0, 0)


def dot(a, b):
    return lax.dot_general(a, b, (((1,), (0,)), ((), ())), preferred_element_type=F32)


def dot_nt(a, b):
    return lax.dot_general(a, b, (((1,), (1,)), ((), ())), preferred_element_type=F32)


def dot_full(a, b):
    return lax.dot_general(
        a, b, (((1,), (0,)), ((), ())), precision=lax.Precision.HIGHEST, preferred_element_type=F32
    )


def split2(x):
    hi = x.astype(BF16)
    return hi, (x - hi.astype(F32)).astype(BF16)


def left_pieces(x):
    hi, lo = split2(x)
    return jnp.concatenate([hi, lo, hi], axis=1)


def ones_where(mask):
    return jnp.where(mask, 1.0, 0.0).astype(BF16)


def kernel(
    n_slab,
    n_sub,
    adjoint_in,
    scale_in,
    cluster_in,
    links_in,
    list_in,
    k_in,
    self_in,
    neighbour_in,
    out_ref,
    adjoint_ref,
    scale_ref,
    cluster_ref,
    links_ref,
    list_ref,
    k_ref,
    self_ref,
    neighbour_ref,
    x_ref,
    h_ref,
    p_ref,
    state_ref,
    factor_ref,
    linkb_ref,
    own_m_ref,
    halo_m_ref,
    last_m_ref,
    g_own_ref,
    g_halo_ref,
    kk_ref,
    nn_ref,
    ns_ref,
    pad_ref,
    before_ref,
    pre_ref,
    send_ref,
    recv_ref,
    id_send_ref,
    id_recv_ref,
    in_sem,
    send_sem,
    recv_sem,
    id_send_sem,
    id_recv_sem,
):
    dofs, elems = adjoint_ref.shape
    side = elems // 4
    per = 4 * CAP
    half = per // 2
    slots = 3 * per
    count = len(LEVELS)

    def fetch(n, src, dst):
        copy = pltpu.make_async_copy(src, dst, in_sem.at[n])
        copy.start()
        return copy

    list_copy = fetch(0, list_in, list_ref)
    cluster_copy = fetch(1, cluster_in, cluster_ref)
    k_copy = fetch(2, k_in, k_ref)
    adjoint_copy = fetch(3, adjoint_in, adjoint_ref)
    scale_copy = fetch(4, scale_in, scale_ref)
    links_copy = fetch(5, links_in, links_ref)
    neighbour_copy = fetch(6, neighbour_in, neighbour_ref)
    self_copy = fetch(7, self_in, self_ref)

    i = lax.axis_index("slab")
    j = lax.axis_index("sub")
    low = ((i - 1, j), (i, j - 1))
    has_low = (i > 0, j > 0)
    high = ((i + 1, j), (i, j + 1))
    has_high = (i < n_slab - 1, j < n_sub - 1)
    target = (low[0], high[0], low[1], high[1])
    has_target = (has_low[0], has_high[0], has_low[1], has_high[1])
    has_source = (has_high[0], has_low[0], has_high[1], has_low[1])
    link_base = (elems + side, elems, elems + 3 * side, elems + 2 * side)

    barrier = pltpu.get_barrier_semaphore()
    for h in range(4):

        @pl.when(has_target[h])
        def _(h=h):
            pl.semaphore_signal(barrier, inc=1, device_id=target[h], device_id_type=MESH)

    def wave(k, h):
        return pltpu.make_async_remote_copy(
            src_ref=send_ref.at[k, pl.ds(h * CAP, CAP)],
            dst_ref=recv_ref.at[k, pl.ds(h * CAP, CAP)],
            send_sem=send_sem.at[k, h],
            recv_sem=recv_sem.at[k, h],
            device_id=target[h],
            device_id_type=MESH,
        )

    def id_wave(c, h):
        return pltpu.make_async_remote_copy(
            src_ref=id_send_ref.at[c],
            dst_ref=id_recv_ref.at[c, h],
            send_sem=id_send_sem.at[c, h],
            recv_sem=id_recv_sem.at[c, h],
            device_id=target[h],
            device_id_type=MESH,
        )

    def each(has, do, sides=(2, 3, 0, 1)):
        for h in sides:

            @pl.when(has[h])
            def _(h=h):
                do(h)

    for h in range(4):

        @pl.when(jnp.logical_not(has_source[h]))
        def _(h=h):
            recv_ref[:, h * CAP : (h + 1) * CAP, :] = jnp.zeros((count, CAP, LANES), F32)
            id_recv_ref[:, h] = jnp.full((3,) + id_recv_ref.shape[2:], -1.0, F32)

    before_from = lax.broadcasted_iota(jnp.int32, (elems, elems), 0)
    before_to = lax.broadcasted_iota(jnp.int32, (elems, elems), 1)
    before_ref[...] = ones_where(
        (before_from < before_to) & (before_from // side == before_to // side)
    )
    pad_ref[...] = jnp.zeros_like(pad_ref)
    kk_ref[...] = jnp.zeros_like(kk_ref)
    x_ref[...] = jnp.zeros_like(x_ref)
    id_send_ref[...] = jnp.full(id_send_ref.shape, -1.0, F32)
    state_ref[slots:, :] = jnp.zeros((state_ref.shape[0] - slots, LANES), F32)
    p_ref[slots:, :] = jnp.zeros((p_ref.shape[0] - slots, elems), BF16)

    list_copy.wait()
    cluster_copy.wait()
    k_copy.wait()
    adjoint_copy.wait()
    scale_copy.wait()
    links_copy.wait()

    listed = jnp.concatenate([list_ref[0:1, :], list_ref[1:2, :]], axis=1)
    h_ref[...] = ones_where(lax.broadcasted_iota(jnp.int32, (elems, elems), 0) == listed)

    cluster8 = jnp.broadcast_to(cluster_ref[...].astype(F32), (16, elems)).astype(BF16)
    cluster_p = dot(cluster8, h_ref[...])
    level_row = lax.broadcasted_iota(jnp.int32, (16, elems), 0).astype(F32)
    is_level = cluster_p == level_row
    ranks = dot(ones_where(is_level), before_ref[...])
    rank = jnp.sum(jnp.where(is_level, ranks, 0.0), axis=0, keepdims=True)
    position = lax.broadcasted_iota(jnp.int32, (1, elems), 1)
    side_of = position // side
    slot = (cluster_p[0:1, :] * per + rank).astype(jnp.int32) + side_of * CAP

    base = jnp.where(
        side_of == 0,
        link_base[0],
        jnp.where(side_of == 1, link_base[1], jnp.where(side_of == 2, link_base[2], link_base[3])),
    )
    own_plus = listed + 1
    far_plus = base + (position - side_of * side) + 1
    id_rows = jnp.concatenate(
        [
            (own_plus // 32 * 32).astype(F32),
            (own_plus % 32).astype(F32),
            (far_plus // 32 * 32).astype(F32),
            (far_plus % 32).astype(F32),
            jnp.zeros((12, elems), F32),
        ],
        axis=0,
    ).astype(BF16)

    def step_size(c):
        return TIME_STEP * 2.0**c

    def rows_of(c):
        return slice(c * per, (c + 1) * per)

    aux = jnp.concatenate(
        [scale_ref[...], links_ref[...].astype(F32), jnp.zeros((11, elems), F32)], axis=0
    )
    for at, part in ((0, adjoint_ref[...]), (dofs, aux)):
        hi, lo = split2(part)
        x_ref[at : at + part.shape[0], :] = hi
        x_ref[LANES + at : LANES + at + part.shape[0], :] = lo

    own_ids = {}

    def place(c):
        rows = rows_of(c)
        q = ones_where(lax.broadcasted_iota(jnp.int32, (per, elems), 0) + c * per == slot)
        ids = dot_nt(id_rows, q)
        own = ids[0:1, :] + ids[1:2, :] - 1.0
        own_ids[c] = jnp.concatenate([own, own], axis=1)
        id_send_ref[c, 0:1, 0:per] = ids[2:3, :] + ids[3:4, :] - 1.0
        p = dot_nt(q, h_ref[...]).astype(BF16)
        p_ref[rows, :] = p
        placed = dot_nt(p, x_ref[...])
        placed = placed[:, 0:LANES] + placed[:, LANES:]
        lane = lax.broadcasted_iota(jnp.int32, (per, LANES), 1)
        state_ref[rows, :] = jnp.where(lane < dofs, placed, 0.0)
        factor_ref[rows, :] = jnp.broadcast_to(placed[:, dofs : dofs + 1], (per, LANES))
        return placed

    def spread_links(c, placed):
        rows = rows_of(c)
        lane = lax.broadcasted_iota(jnp.int32, (per, LANES), 1)
        faces = [
            jnp.broadcast_to(placed[:, dofs + 1 + f : dofs + 2 + f], (per, LANES)) for f in range(4)
        ]
        linkb_ref[0, rows, :] = faces[0]
        linkb_ref[1, rows, :] = jnp.where(lane < LANES // 2, faces[0], faces[1])
        linkb_ref[2, rows, :] = faces[1]
        linkb_ref[3, rows, :] = faces[2]
        linkb_ref[4, rows, :] = jnp.where(lane < LANES // 2, faces[2], faces[3])
        linkb_ref[5, rows, :] = faces[3]
        for block in range(3):
            cut = half - block * (LANES - half)
            linkb_ref[6 + block, rows, :] = jnp.where(lane < cut, faces[block], faces[block + 1])

    def put(ref, at, matrix):
        hi, lo = split2(matrix)
        cols = slice(at * LANES, (at + 1) * LANES)
        ref[0:LANES, cols] = hi
        ref[LANES : 2 * LANES, cols] = hi
        ref[2 * LANES :, cols] = lo

    pad_ref[0, 0:dofs, 0:dofs] = k_ref[...]
    k1 = pad_ref[0].T
    k2 = dot_full(k1, k1)
    k3 = dot_full(k2, k1)
    for at, matrix in enumerate((k1, k2, k3)):
        put(kk_ref, at, matrix)

    def predict(k):
        c = LEVELS[k]
        v = state_ref[rows_of(c), :]
        terms = dot(left_pieces(v), kk_ref[...])
        a = step_size(c) * factor_ref[rows_of(c), :]
        send_ref[k] = (
            v
            + a * (1.0 / 2.0) * terms[:, 0:LANES]
            + a * a * (1.0 / 6.0) * terms[:, LANES : 2 * LANES]
            + a * a * a * (1.0 / 24.0) * terms[:, 2 * LANES :]
        )

    def send(k):
        each(has_target, lambda h: wave(k, h).start())

    def build(m_ref, c, col, links_at, blocks, ids):
        for block in range(blocks):
            row = ids[:, block % 3 * LANES : (block % 3 + 1) * LANES]
            at = (col + block) * LANES
            m_ref[c, :, at : at + LANES] = ones_where(linkb_ref[links_at + block, 0:slots, :] == row)

    def spread(g_ref, at, product):
        size = product.shape[0]
        for f in range(4):
            hi, lo = split2(product[:, f * LANES : (f + 1) * LANES])
            rows = slice(at + f * size, at + (f + 1) * size)
            g_ref[rows, 0:LANES] = hi
            g_ref[rows, LANES : 2 * LANES] = lo

    def gather(m, g):
        both = dot(m, g)
        return both[:, 0:LANES] + both[:, LANES:]

    def add(c, d, change):
        a = step_size(c) * factor_ref[rows_of(d), :]
        state_ref[rows_of(d), :] += a * change

    def halo_ids(c):
        lane = lax.broadcasted_iota(jnp.int32, (1, 2 * LANES), 1)
        ids = [id_recv_ref[c, h, 0:1, :] for h in range(4)]
        return jnp.where(
            lane < CAP,
            ids[0],
            jnp.where(lane < 2 * CAP, ids[1], jnp.where(lane < 3 * CAP, ids[2], ids[3])),
        )

    first = LEVELS[0]
    placed = {first: place(first)}
    predict(0)
    pl.semaphore_wait(barrier, sum(has.astype(jnp.int32) for has in has_target))
    each(has_target, lambda h: id_wave(first, h).start())
    send(0)

    for c in (1, 0):
        placed[c] = place(c)
    each(has_target, lambda h: id_wave(1, h).start())
    each(has_target, lambda h: id_wave(0, h).start())
    for c in (2, 1, 0):
        spread_links(c, placed[c])

    neighbour_copy.wait()
    self_copy.wait()
    pad_ref[1, 0:dofs, 0:dofs] = self_ref[...]
    for f in range(4):
        pad_ref[2 + f, 0:dofs, 0:dofs] = neighbour_ref[:, f * dofs : (f + 1) * dofs]
    for f in range(4):
        put(nn_ref, f, pad_ref[2 + f].T)
        hi, lo = split2(pad_ref[2 + f, 0:dofs, :])
        ns_ref[f * dofs : (f + 1) * dofs, :] = jnp.concatenate([hi, hi, lo], axis=1)
    put(nn_ref, 4, pad_ref[1].T)

    seen = set()
    for k, c in enumerate(LEVELS):
        last = k == count - 1
        if c not in seen:
            build(own_m_ref, c, 0, 0, 6, own_ids[c])
        product = dot(left_pieces(send_ref[k]), nn_ref[...])
        spread(g_own_ref, 0, product)
        for d in range(3):
            change = gather(own_m_ref[c, rows_of(d), :], g_own_ref[...])
            if d == c:
                change = change + product[:, 4 * LANES :]
            add(c, d, change)
        if c not in seen:
            seen.add(c)
            each(has_source, lambda h, c=c: id_wave(c, h).wait_recv())
            ids = halo_ids(c)
            for part in range(2):
                cut = ids[:, part * half : (part + 1) * half]
                build(halo_m_ref, c, 3 * part, 6, 3, jnp.concatenate([cut] * 4, axis=1))
        if last:
            ids = halo_ids(c)
            for block in range(2):
                size = min(LANES, per - block * LANES)
                row = ids[:, block * LANES : (block + 1) * LANES]
                column = jnp.broadcast_to(row, (LANES, LANES)).T
                column = jnp.concatenate([column] * 4, axis=1)[0:size, :]
                for f in range(4):
                    row = links_ref[f : f + 1, :].astype(F32)
                    last_m_ref[f, block * LANES : block * LANES + size, :] = ones_where(column == row)
            turned = jnp.concatenate(
                [state_ref[at * LANES : (at + 1) * LANES, :].T for at in range(5)], axis=1
            )
            both = dot(jnp.concatenate(split2(turned), axis=0), p_ref[...])
            pre_ref[...] = (both[0:LANES] + both[LANES:])[0:dofs, :]
            each(has_source, lambda h, k=k: wave(k, h).wait_recv())
            product = dot_nt(ns_ref[...], left_pieces(recv_ref[k]))
            total = jnp.zeros((2 * dofs, elems), F32)
            for f in range(4):
                pieces = split2(product[f * dofs : (f + 1) * dofs, :])
                total = total + dot(jnp.concatenate(pieces, axis=0), last_m_ref[f])
            a = step_size(c) * scale_ref[...]
            out_ref[...] = pre_ref[...] + a * (total[0:dofs] + total[dofs:])
        else:
            then = LEVELS[k + 1]
            rest = [d for d in range(3) if d != then]
            wide = 2 * per
            each(has_source, lambda h, k=k: wave(k, h).wait_recv(), (0, 1))
            product = dot(left_pieces(recv_ref[k, 0:half, :]), nn_ref[:, 0 : 4 * LANES])
            spread(g_halo_ref, 0, product)
            add(c, then, gather(halo_m_ref[c, rows_of(then), 0:wide], g_halo_ref[0:wide, :]))
            each(has_source, lambda h, k=k: wave(k, h).wait_recv(), (2, 3))
            product = dot(left_pieces(recv_ref[k, half:per, :]), nn_ref[:, 0 : 4 * LANES])
            spread(g_halo_ref, wide, product)
            add(c, then, gather(halo_m_ref[c, rows_of(then), wide:], g_halo_ref[wide:, :]))
            predict(k + 1)
            send(k + 1)
            for d in rest:
                add(c, d, gather(halo_m_ref[c, rows_of(d), :], g_halo_ref[...]))

    for c in range(3):
        each(has_target, lambda h, c=c: id_wave(c, h).wait_send())
    for k in range(count):
        each(has_target, lambda h, k=k: wave(k, h).wait_send())


def shards(n_slab, n_sub, adjoint, elem_scale, cluster, face_links, halo_list, k_matrix, w_self, w_neighbour):
    dofs, elems = adjoint.shape
    per = 4 * CAP
    slots = 3 * per
    padded = 5 * LANES
    count = len(LEVELS)
    operands = (
        adjoint,
        elem_scale.reshape(1, elems),
        cluster.reshape(1, elems),
        face_links,
        halo_list,
        k_matrix,
        w_self,
        w_neighbour,
    )
    return pl.pallas_call(
        functools.partial(kernel, n_slab, n_sub),
        out_shape=jax.ShapeDtypeStruct((dofs, elems), F32),
        in_specs=[pl.BlockSpec(memory_space=pltpu.HBM)] * 8,
        out_specs=pl.BlockSpec(memory_space=pltpu.VMEM),
        scratch_shapes=[pltpu.VMEM(x.shape, x.dtype) for x in operands]
        + [
            pltpu.VMEM((2 * LANES, elems), BF16),
            pltpu.VMEM((elems, elems), BF16),
            pltpu.VMEM((padded, elems), BF16),
            pltpu.VMEM((padded, LANES), F32),
            pltpu.VMEM((slots, LANES), F32),
            pltpu.VMEM((9, slots, LANES), F32),
            pltpu.VMEM((3, slots, 4 * per), BF16),
            pltpu.VMEM((3, slots, 4 * per), BF16),
            pltpu.VMEM((4, per, elems), BF16),
            pltpu.VMEM((4 * per, 2 * LANES), BF16),
            pltpu.VMEM((4 * per, 2 * LANES), BF16),
            pltpu.VMEM((3 * LANES, 3 * LANES), BF16),
            pltpu.VMEM((3 * LANES, 5 * LANES), BF16),
            pltpu.VMEM((4 * dofs, 3 * LANES), BF16),
            pltpu.VMEM((6, LANES, LANES), F32),
            pltpu.VMEM((elems, elems), BF16),
            pltpu.VMEM((dofs, elems), F32),
            pltpu.VMEM((count, per, LANES), F32),
            pltpu.VMEM((count, per, LANES), F32),
            pltpu.VMEM((3, 8, 2 * LANES), F32),
            pltpu.VMEM((3, 4, 8, 2 * LANES), F32),
            pltpu.SemaphoreType.DMA((8,)),
            pltpu.SemaphoreType.DMA((count, 4)),
            pltpu.SemaphoreType.DMA((count, 4)),
            pltpu.SemaphoreType.DMA((3, 4)),
            pltpu.SemaphoreType.DMA((3, 4)),
        ],
        compiler_params=pltpu.CompilerParams(
            collective_id=0, has_side_effects=True, vmem_limit_bytes=58 * 1024 * 1024
        ),
    )(*operands)


def solution(mesh):
    placed = (
        P(None, ("slab", "sub")),
        P(("slab", "sub")),
        P(("slab", "sub")),
        P(None, ("slab", "sub")),
        P(None, ("slab", "sub")),
        P(),
        P(),
        P(),
    )
    return jax.shard_map(
        functools.partial(shards, mesh.shape["slab"], mesh.shape["sub"]),
        mesh=mesh,
        in_specs=placed,
        out_specs=P(None, ("slab", "sub")),
        check_vma=False,
    )
```

time: 49.1 us -> 45.5 us (0.927)
  local copies, waits for them, and re-layouts: 6.78 us -> 1.59 us
  Pallas kernels: 41.9 us -> 43.7 us
    unnamed x17 -> x1, local copies, waits for them, and re-layouts: 6.78 us -> 1.59 us
    pallas_call x1, Pallas kernels: 41.9 us -> 43.7 us  [shards(): pl.pallas_call(functools.partial(kernel, n_slab, n_sub), out_shape=jax.Sh...]
where the time goes in v2:
time: 45.5 us; the launch traced here: 45.3 us
  Pallas kernels  43.7 us (96%)
  local copies, waits for them, and re-layouts  1.59 us (3%)
    pallas_call x1, Pallas kernels, shards(): pl.pallas_call(functools.partial(kernel, n_slab, n_sub), out_shape=jax.Sh...  43.7 us
    unnamed x1, local copies, waits for them, and re-layouts  1.59 us

profile of v2, /device:TPU:24, one launch (start us, length us, event | category | flops | bytes accessed | tf_op | source)
XLA Modules:
  0.0 45.3 jit_solution(2503832168301907157)
XLA Ops:
  0.0 43.7 %shard_map.82 = f32[80,512]{1,0:T(8,128)} custom-call(f32[80,512]{1,0:T(8,128)} %adjoint_in.1, f32[1,512]{1,0:T(1,128)} %bitcast.2, s32[1,512]{1,0:T(1,128)} %bitcast.3, s32[4,512]{1,0:T(4,128)} %links_in.1, s32[2,256]{1,0:T(2,128)} %list_in.1, f32[80,80]{1,0:T(8,128)} %k_in.1, f32[80,80]{1,0:T(8,128)} %self_in.1, f32[80,320]{1,0:T(8,128)} %neighbour_in.1), custom_call_target="tpu_custom_call" | custom-call | tf_op jit(solution)/shard_map/pallas_call | solution.py:432
  43.7 1.6 %copy.10 = f32[80,512]{1,0:T(8,128)} copy(f32[80,512]{1,0:T(8,128)} %shard_map.82) | data formatting | bytes 327680

commit v3 on v2

--- a/solution.py
+++ b/solution.py
@@ -14,6 +14,8 @@
 TIME_STEP = 0.125
 CAP = 48
 LANES = 128
+PACKED = 32
+SPARE = CAP - PACKED
 LEVELS = (2, 1, 0, 0, 1, 0, 0)
 
 
@@ -66,10 +68,13 @@
     self_ref,
     neighbour_ref,
     x_ref,
+    moved_ref,
     h_ref,
+    q_ref,
     p_ref,
     state_ref,
     factor_ref,
+    powers_ref,
     linkb_ref,
     own_m_ref,
     halo_m_ref,
@@ -83,6 +88,7 @@
     before_ref,
     pre_ref,
     send_ref,
+    pack_ref,
     recv_ref,
     id_send_ref,
     id_recv_ref,
@@ -132,11 +138,12 @@
             pl.semaphore_signal(barrier, inc=1, device_id=target[h], device_id_type=MESH)
 
     def wave(k, h):
+        at = pl.ds(h * PACKED, PACKED)
         return pltpu.make_async_remote_copy(
-            src_ref=send_ref.at[k, pl.ds(h * CAP, CAP)],
-            dst_ref=recv_ref.at[k, pl.ds(h * CAP, CAP)],
-            send_sem=send_sem.at[k, h],
-            recv_sem=recv_sem.at[k, h],
+            src_ref=pack_ref.at[k, at],
+            dst_ref=recv_ref.at[k, at],
+            send_sem=send_sem.at[h],
+            recv_sem=recv_sem.at[k % 2, h],
             device_id=target[h],
             device_id_type=MESH,
         )
@@ -162,11 +169,11 @@
 
         @pl.when(jnp.logical_not(has_source[h]))
         def _(h=h):
-            recv_ref[:, h * CAP : (h + 1) * CAP, :] = jnp.zeros((count, CAP, LANES), F32)
+            recv_ref[:, h * PACKED : (h + 1) * PACKED, :] = jnp.zeros((count, PACKED, LANES), F32)
             id_recv_ref[:, h] = jnp.full((3,) + id_recv_ref.shape[2:], -1.0, F32)
 
-    before_from = lax.broadcasted_iota(jnp.int32, (elems, elems), 0)
-    before_to = lax.broadcasted_iota(jnp.int32, (elems, elems), 1)
+    before_from = lax.broadcasted_iota(jnp.int32, (2 * side, 2 * side), 0)
+    before_to = lax.broadcasted_iota(jnp.int32, (2 * side, 2 * side), 1)
     before_ref[...] = ones_where(
         (before_from < before_to) & (before_from // side == before_to // side)
     )
@@ -187,15 +194,34 @@
     listed = jnp.concatenate([list_ref[0:1, :], list_ref[1:2, :]], axis=1)
     h_ref[...] = ones_where(lax.broadcasted_iota(jnp.int32, (elems, elems), 0) == listed)
 
+    aux = jnp.concatenate(
+        [scale_ref[...], links_ref[...].astype(F32), jnp.zeros((11, elems), F32)], axis=0
+    )
+    for at, part in ((0, adjoint_ref[...]), (dofs, aux)):
+        hi, lo = split2(part)
+        x_ref[at : at + part.shape[0], :] = hi
+        x_ref[LANES + at : LANES + at + part.shape[0], :] = lo
+
     cluster8 = jnp.broadcast_to(cluster_ref[...].astype(F32), (16, elems)).astype(BF16)
-    cluster_p = dot(cluster8, h_ref[...])
+    by_position = dot(jnp.concatenate([cluster8, x_ref[...]], axis=0), h_ref[...])
+    cluster_p = by_position[0:16, :]
+    moved_ref[...] = by_position[16:, :].astype(BF16)
+
     level_row = lax.broadcasted_iota(jnp.int32, (16, elems), 0).astype(F32)
     is_level = cluster_p == level_row
-    ranks = dot(ones_where(is_level), before_ref[...])
+    marks = ones_where(is_level)
+    ranks = jnp.concatenate(
+        [dot(marks[:, 0 : 2 * side], before_ref[...]), dot(marks[:, 2 * side :], before_ref[...])],
+        axis=1,
+    )
     rank = jnp.sum(jnp.where(is_level, ranks, 0.0), axis=0, keepdims=True)
     position = lax.broadcasted_iota(jnp.int32, (1, elems), 1)
     side_of = position // side
-    slot = (cluster_p[0:1, :] * per + rank).astype(jnp.int32) + side_of * CAP
+    rank = rank.astype(jnp.int32)
+    within = jnp.where(
+        rank < PACKED, 4 * SPARE + side_of * PACKED + rank, side_of * SPARE + rank - PACKED
+    )
+    slot = cluster_p[0:1, :].astype(jnp.int32) * per + within
 
     base = jnp.where(
         side_of == 0,
@@ -221,14 +247,6 @@
     def rows_of(c):
         return slice(c * per, (c + 1) * per)
 
-    aux = jnp.concatenate(
-        [scale_ref[...], links_ref[...].astype(F32), jnp.zeros((11, elems), F32)], axis=0
-    )
-    for at, part in ((0, adjoint_ref[...]), (dofs, aux)):
-        hi, lo = split2(part)
-        x_ref[at : at + part.shape[0], :] = hi
-        x_ref[LANES + at : LANES + at + part.shape[0], :] = lo
-
     own_ids = {}
 
     def place(c):
@@ -237,14 +255,18 @@
         ids = dot_nt(id_rows, q)
         own = ids[0:1, :] + ids[1:2, :] - 1.0
         own_ids[c] = jnp.concatenate([own, own], axis=1)
-        id_send_ref[c, 0:1, 0:per] = ids[2:3, :] + ids[3:4, :] - 1.0
-        p = dot_nt(q, h_ref[...]).astype(BF16)
-        p_ref[rows, :] = p
-        placed = dot_nt(p, x_ref[...])
+        id_send_ref[c, :, 0:per] = ids[2:3, :] + ids[3:4, :] - 1.0
+        q_ref[rows, :] = q
+        placed = dot_nt(q, moved_ref[...])
         placed = placed[:, 0:LANES] + placed[:, LANES:]
         lane = lax.broadcasted_iota(jnp.int32, (per, LANES), 1)
         state_ref[rows, :] = jnp.where(lane < dofs, placed, 0.0)
-        factor_ref[rows, :] = jnp.broadcast_to(placed[:, dofs : dofs + 1], (per, LANES))
+        factor = jnp.broadcast_to(placed[:, dofs : dofs + 1], (per, LANES))
+        factor_ref[rows, :] = factor
+        a = step_size(c) * factor
+        powers_ref[0, rows, :] = a * (1.0 / 2.0)
+        powers_ref[1, rows, :] = a * a * (1.0 / 6.0)
+        powers_ref[2, rows, :] = a * a * a * (1.0 / 24.0)
         return placed
 
     def spread_links(c, placed):
@@ -279,18 +301,48 @@
 
     def predict(k):
         c = LEVELS[k]
-        v = state_ref[rows_of(c), :]
+        rows = rows_of(c)
+        v = state_ref[rows, :]
         terms = dot(left_pieces(v), kk_ref[...])
-        a = step_size(c) * factor_ref[rows_of(c), :]
-        send_ref[k] = (
-            v
-            + a * (1.0 / 2.0) * terms[:, 0:LANES]
-            + a * a * (1.0 / 6.0) * terms[:, LANES : 2 * LANES]
-            + a * a * a * (1.0 / 24.0) * terms[:, 2 * LANES :]
-        )
+        w = v
+        for n in range(3):
+            w = w + powers_ref[n, rows, :] * terms[:, n * LANES : (n + 1) * LANES]
+        send_ref[k] = w
+        lane = lax.broadcasted_iota(jnp.int32, (SPARE, LANES), 1)
+        for h in range(4):
+            bottom = w[h * SPARE : (h + 1) * SPARE]
+            for m, shift in enumerate((dofs, dofs - CAP)):
+                at = h * PACKED + m * SPARE
+                top = w[4 * SPARE + at : 4 * SPARE + at + SPARE]
+                pack_ref[k, at : at + SPARE, :] = jnp.where(
+                    lane < dofs, top, pltpu.roll(bottom, shift, 1)
+                )
+
+    def unpacked(k, sides):
+        lane = lax.broadcasted_iota(jnp.int32, (SPARE, LANES), 1)
+        rows = [recv_ref[k, sides[0] * PACKED : (sides[-1] + 1) * PACKED, :]]
+        for h in sides:
+            first = recv_ref[k, h * PACKED : h * PACKED + SPARE, :]
+            second = recv_ref[k, h * PACKED + SPARE : (h + 1) * PACKED, :]
+            rows.append(
+                jnp.where(
+                    lane < LANES - dofs,
+                    pltpu.roll(first, LANES - dofs, 1),
+                    pltpu.roll(second, LANES - dofs + CAP, 1),
+                )
+            )
+        return jnp.concatenate(rows, axis=0)
+
+    even = lax.rem(i, 2) == 0
+    off_chip = tuple(jnp.logical_and(has_target[h], even if h == 0 else jnp.logical_not(even)) for h in range(2))
+    on_chip = tuple(jnp.logical_and(has_target[h], jnp.logical_not(even) if h == 0 else even) for h in range(2))
 
     def send(k):
-        each(has_target, lambda h: wave(k, h).start())
+        start = lambda h: wave(k, h).start()
+        each(off_chip, start, (1,))
+        each(has_target, start, (2, 3))
+        each(off_chip, start, (0,))
+        each(on_chip, start, (0, 1))
 
     def build(m_ref, c, col, links_at, blocks, ids):
         for block in range(blocks):
@@ -310,17 +362,17 @@
         both = dot(m, g)
         return both[:, 0:LANES] + both[:, LANES:]
 
-    def add(c, d, change):
-        a = step_size(c) * factor_ref[rows_of(d), :]
-        state_ref[rows_of(d), :] += a * change
+    def add(c, rows, change):
+        state_ref[rows, :] += step_size(c) * factor_ref[rows, :] * change
 
     def halo_ids(c):
         lane = lax.broadcasted_iota(jnp.int32, (1, 2 * LANES), 1)
-        ids = [id_recv_ref[c, h, 0:1, :] for h in range(4)]
+        side_at = jnp.where(lane < 4 * SPARE, lane // SPARE, (lane - 4 * SPARE) // PACKED)
+        ids = [id_recv_ref[c, h] for h in range(4)]
         return jnp.where(
-            lane < CAP,
+            side_at == 0,
             ids[0],
-            jnp.where(lane < 2 * CAP, ids[1], jnp.where(lane < 3 * CAP, ids[2], ids[3])),
+            jnp.where(side_at == 1, ids[1], jnp.where(side_at == 2, ids[2], ids[3])),
         )
 
     first = LEVELS[0]
@@ -359,19 +411,29 @@
             change = gather(own_m_ref[c, rows_of(d), :], g_own_ref[...])
             if d == c:
                 change = change + product[:, 4 * LANES :]
-            add(c, d, change)
+            add(c, rows_of(d), change)
         if c not in seen:
             seen.add(c)
             each(has_source, lambda h, c=c: id_wave(c, h).wait_recv())
             ids = halo_ids(c)
             for part in range(2):
-                cut = ids[:, part * half : (part + 1) * half]
-                build(halo_m_ref, c, 3 * part, 6, 3, jnp.concatenate([cut] * 4, axis=1))
+                tops = 4 * SPARE + 2 * part * PACKED
+                cut = [
+                    ids[:, tops : tops + 2 * PACKED],
+                    ids[:, 2 * part * SPARE : 2 * (part + 1) * SPARE],
+                ]
+                build(halo_m_ref, c, 3 * part, 6, 3, jnp.concatenate(cut * 4, axis=1))
+        each(has_target, lambda h, k=k: wave(k, h).wait_send())
+        if k in (1, 2, 3):
+            each(has_target, lambda h, k=k: id_wave(k - 1, h).wait_send())
+        if k == 3:
+            p_ref[0:slots, :] = dot_nt(q_ref[...], h_ref[...]).astype(BF16)
         if last:
             ids = halo_ids(c)
             for block in range(2):
                 size = min(LANES, per - block * LANES)
-                row = ids[:, block * LANES : (block + 1) * LANES]
+                at = 4 * SPARE * (1 - block)
+                row = ids[:, at : at + LANES]
                 column = jnp.broadcast_to(row, (LANES, LANES)).T
                 column = jnp.concatenate([column] * 4, axis=1)[0:size, :]
                 for f in range(4):
@@ -383,7 +445,8 @@
             both = dot(jnp.concatenate(split2(turned), axis=0), p_ref[...])
             pre_ref[...] = (both[0:LANES] + both[LANES:])[0:dofs, :]
             each(has_source, lambda h, k=k: wave(k, h).wait_recv())
-            product = dot_nt(ns_ref[...], left_pieces(recv_ref[k]))
+            got = unpacked(k, (0, 1, 2, 3))
+            product = dot_nt(ns_ref[...], left_pieces(got))
             total = jnp.zeros((2 * dofs, elems), F32)
             for f in range(4):
                 pieces = split2(product[f * dofs : (f + 1) * dofs, :])
@@ -394,23 +457,17 @@
             then = LEVELS[k + 1]
             rest = [d for d in range(3) if d != then]
             wide = 2 * per
-            each(has_source, lambda h, k=k: wave(k, h).wait_recv(), (0, 1))
-            product = dot(left_pieces(recv_ref[k, 0:half, :]), nn_ref[:, 0 : 4 * LANES])
-            spread(g_halo_ref, 0, product)
-            add(c, then, gather(halo_m_ref[c, rows_of(then), 0:wide], g_halo_ref[0:wide, :]))
-            each(has_source, lambda h, k=k: wave(k, h).wait_recv(), (2, 3))
-            product = dot(left_pieces(recv_ref[k, half:per, :]), nn_ref[:, 0 : 4 * LANES])
-            spread(g_halo_ref, wide, product)
-            add(c, then, gather(halo_m_ref[c, rows_of(then), wide:], g_halo_ref[wide:, :]))
+            for part, sides in enumerate(((0, 1), (2, 3))):
+                each(has_source, lambda h, k=k: wave(k, h).wait_recv(), sides)
+                got = unpacked(k, sides)
+                product = dot(left_pieces(got), nn_ref[:, 0 : 4 * LANES])
+                at = slice(part * wide, (part + 1) * wide)
+                spread(g_halo_ref, part * wide, product)
+                add(c, rows_of(then), gather(halo_m_ref[c, rows_of(then), at], g_halo_ref[at, :]))
             predict(k + 1)
             send(k + 1)
             for d in rest:
-                add(c, d, gather(halo_m_ref[c, rows_of(d), :], g_halo_ref[...]))
-
-    for c in range(3):
-        each(has_target, lambda h, c=c: id_wave(c, h).wait_send())
-    for k in range(count):
-        each(has_target, lambda h, k=k: wave(k, h).wait_send())
+                add(c, rows_of(d), gather(halo_m_ref[c, rows_of(d), :], g_halo_ref[...]))
 
 
 def shards(n_slab, n_sub, adjoint, elem_scale, cluster, face_links, halo_list, k_matrix, w_self, w_neighbour):
@@ -437,10 +494,13 @@
         scratch_shapes=[pltpu.VMEM(x.shape, x.dtype) for x in operands]
         + [
             pltpu.VMEM((2 * LANES, elems), BF16),
+            pltpu.VMEM((2 * LANES, elems), BF16),
             pltpu.VMEM((elems, elems), BF16),
+            pltpu.VMEM((slots, elems), BF16),
             pltpu.VMEM((padded, elems), BF16),
             pltpu.VMEM((padded, LANES), F32),
             pltpu.VMEM((slots, LANES), F32),
+            pltpu.VMEM((3, slots, LANES), F32),
             pltpu.VMEM((9, slots, LANES), F32),
             pltpu.VMEM((3, slots, 4 * per), BF16),
             pltpu.VMEM((3, slots, 4 * per), BF16),
@@ -451,15 +511,16 @@
             pltpu.VMEM((3 * LANES, 5 * LANES), BF16),
             pltpu.VMEM((4 * dofs, 3 * LANES), BF16),
             pltpu.VMEM((6, LANES, LANES), F32),
-            pltpu.VMEM((elems, elems), BF16),
+            pltpu.VMEM((elems // 2, elems // 2), BF16),
             pltpu.VMEM((dofs, elems), F32),
             pltpu.VMEM((count, per, LANES), F32),
-            pltpu.VMEM((count, per, LANES), F32),
-            pltpu.VMEM((3, 8, 2 * LANES), F32),
-            pltpu.VMEM((3, 4, 8, 2 * LANES), F32),
+            pltpu.VMEM((count, 4 * PACKED, LANES), F32),
+            pltpu.VMEM((count, 4 * PACKED, LANES), F32),
+            pltpu.VMEM((3, 1, 2 * LANES), F32),
+            pltpu.VMEM((3, 4, 1, 2 * LANES), F32),
             pltpu.SemaphoreType.DMA((8,)),
-            pltpu.SemaphoreType.DMA((count, 4)),
-            pltpu.SemaphoreType.DMA((count, 4)),
+            pltpu.SemaphoreType.DMA((4,)),
+            pltpu.SemaphoreType.DMA((2, 4)),
             pltpu.SemaphoreType.DMA((3, 4)),
             pltpu.SemaphoreType.DMA((3, 4)),
         ],

time: 45.5 us -> 45.1 us (level)
  no operation moved by 1% of the time
where the time goes in v3:
time: 45.1 us; the launch traced here: 44.9 us
  Pallas kernels  43.3 us (96%)
  local copies, waits for them, and re-layouts  1.59 us (4%)
    pallas_call x1, Pallas kernels, shards(): pl.pallas_call(functools.partial(kernel, n_slab, n_sub), out_shape=jax.Sh...  43.3 us
    unnamed x1, local copies, waits for them, and re-layouts  1.59 us

profile of v3, /device:TPU:24, one launch (start us, length us, event | category | flops | bytes accessed | tf_op | source)
XLA Modules:
  0.0 44.9 jit_solution(1383083808580229482)
XLA Ops:
  0.0 43.3 %shard_map.82 = f32[80,512]{1,0:T(8,128)} custom-call(f32[80,512]{1,0:T(8,128)} %adjoint_in.1, f32[1,512]{1,0:T(1,128)} %bitcast.2, s32[1,512]{1,0:T(1,128)} %bitcast.3, s32[4,512]{1,0:T(4,128)} %links_in.1, s32[2,256]{1,0:T(2,128)} %list_in.1, f32[80,80]{1,0:T(8,128)} %k_in.1, f32[80,80]{1,0:T(8,128)} %self_in.1, f32[80,320]{1,0:T(8,128)} %neighbour_in.1), custom_call_target="tpu_custom_call" | custom-call | tf_op jit(solution)/shard_map/pallas_call | solution.py:489
  43.3 1.6 %copy.10 = f32[80,512]{1,0:T(8,128)} copy(f32[80,512]{1,0:T(8,128)} %shard_map.82) | data formatting | bytes 327680

commit v4 on v3

--- a/solution.py
+++ b/solution.py
@@ -16,6 +16,7 @@
 LANES = 128
 PACKED = 32
 SPARE = CAP - PACKED
+RUN = 32
 LEVELS = (2, 1, 0, 0, 1, 0, 0)
 
 
@@ -318,12 +319,17 @@
                     lane < dofs, top, pltpu.roll(bottom, shift, 1)
                 )
 
-    def unpacked(k, sides):
+    def unpacked(k, part, parts=1):
         lane = lax.broadcasted_iota(jnp.int32, (SPARE, LANES), 1)
-        rows = [recv_ref[k, sides[0] * PACKED : (sides[-1] + 1) * PACKED, :]]
-        for h in sides:
-            first = recv_ref[k, h * PACKED : h * PACKED + SPARE, :]
-            second = recv_ref[k, h * PACKED + SPARE : (h + 1) * PACKED, :]
+        start = part * 2 * PACKED
+
+        def rows_at(at, size):
+            return recv_ref[k, start + at : start + at + size, :]
+
+        rows = [rows_at(0, 2 * PACKED * parts)]
+        for h in range(2 * parts):
+            first = rows_at(h * PACKED, SPARE)
+            second = rows_at(h * PACKED + SPARE, SPARE)
             rows.append(
                 jnp.where(
                     lane < LANES - dofs,
@@ -333,15 +339,23 @@
             )
         return jnp.concatenate(rows, axis=0)
 
+    def off_chip_at(h):
+        return jnp.logical_and(has_target[h], even if h == 0 else jnp.logical_not(even))
+
     even = lax.rem(i, 2) == 0
-    off_chip = tuple(jnp.logical_and(has_target[h], even if h == 0 else jnp.logical_not(even)) for h in range(2))
+    far = jnp.logical_or(
+        jnp.logical_and(has_target[0], lax.rem(i, RUN) == 0),
+        jnp.logical_and(has_target[1], lax.rem(i, RUN) == RUN - 1),
+    )
+    before = tuple(jnp.logical_and(off_chip_at(h), jnp.logical_or(far, h == 1)) for h in range(2))
+    after = tuple(jnp.logical_and(off_chip_at(h), jnp.logical_not(jnp.logical_or(far, h == 1))) for h in range(2))
     on_chip = tuple(jnp.logical_and(has_target[h], jnp.logical_not(even) if h == 0 else even) for h in range(2))
 
     def send(k):
         start = lambda h: wave(k, h).start()
-        each(off_chip, start, (1,))
+        each(before, start, (0, 1))
         each(has_target, start, (2, 3))
-        each(off_chip, start, (0,))
+        each(after, start, (0,))
         each(on_chip, start, (0, 1))
 
     def build(m_ref, c, col, links_at, blocks, ids):
@@ -445,7 +459,7 @@
             both = dot(jnp.concatenate(split2(turned), axis=0), p_ref[...])
             pre_ref[...] = (both[0:LANES] + both[LANES:])[0:dofs, :]
             each(has_source, lambda h, k=k: wave(k, h).wait_recv())
-            got = unpacked(k, (0, 1, 2, 3))
+            got = unpacked(k, 0, 2)
             product = dot_nt(ns_ref[...], left_pieces(got))
             total = jnp.zeros((2 * dofs, elems), F32)
             for f in range(4):
@@ -457,14 +471,18 @@
             then = LEVELS[k + 1]
             rest = [d for d in range(3) if d != then]
             wide = 2 * per
-            for part, sides in enumerate(((0, 1), (2, 3))):
-                each(has_source, lambda h, k=k: wave(k, h).wait_recv(), sides)
-                got = unpacked(k, sides)
-                product = dot(left_pieces(got), nn_ref[:, 0 : 4 * LANES])
-                at = slice(part * wide, (part + 1) * wide)
-                spread(g_halo_ref, part * wide, product)
-                add(c, rows_of(then), gather(halo_m_ref[c, rows_of(then), at], g_halo_ref[at, :]))
-            predict(k + 1)
+
+            def take(parts, k=k, c=c, then=then, wide=wide):
+                for part in parts:
+                    each(has_source, lambda h: wave(k, h).wait_recv(), (2 * part, 2 * part + 1))
+                    product = dot(left_pieces(unpacked(k, part)), nn_ref[:, 0 : 4 * LANES])
+                    spread(g_halo_ref, part * wide, product)
+                    at = slice(part * wide, (part + 1) * wide)
+                    add(c, rows_of(then), gather(halo_m_ref[c, rows_of(then), at], g_halo_ref[at, :]))
+                predict(k + 1)
+
+            pl.when(far)(lambda: take((1, 0)))
+            pl.when(jnp.logical_not(far))(lambda: take((0, 1)))
             send(k + 1)
             for d in rest:
                 add(c, rows_of(d), gather(halo_m_ref[c, rows_of(d), :], g_halo_ref[...]))

time: 45.1 us -> 43.4 us (0.962)
  Pallas kernels: 43.3 us -> 41.7 us
    pallas_call x1, Pallas kernels: 43.3 us -> 41.7 us  [shards(): pl.pallas_call(functools.partial(kernel, n_slab, n_sub), out_shape=jax.Sh...]
where the time goes in v4:
time: 43.4 us; the launch traced here: 43.3 us
  Pallas kernels  41.7 us (96%)
  local copies, waits for them, and re-layouts  1.59 us (4%)
    pallas_call x1, Pallas kernels, shards(): pl.pallas_call(functools.partial(kernel, n_slab, n_sub), out_shape=jax.Sh...  41.7 us
    unnamed x1, local copies, waits for them, and re-layouts  1.59 us

profile of v4, /device:TPU:24, one launch (start us, length us, event | category | flops | bytes accessed | tf_op | source)
XLA Modules:
  0.0 43.3 jit_solution(10979981068383925500)
XLA Ops:
  0.0 41.7 %shard_map.82 = f32[80,512]{1,0:T(8,128)} custom-call(f32[80,512]{1,0:T(8,128)} %adjoint_in.1, f32[1,512]{1,0:T(1,128)} %bitcast.2, s32[1,512]{1,0:T(1,128)} %bitcast.3, s32[4,512]{1,0:T(4,128)} %links_in.1, s32[2,256]{1,0:T(2,128)} %list_in.1, f32[80,80]{1,0:T(8,128)} %k_in.1, f32[80,80]{1,0:T(8,128)} %self_in.1, f32[80,320]{1,0:T(8,128)} %neighbour_in.1), custom_call_target="tpu_custom_call" | custom-call | tf_op jit(solution)/shard_map/pallas_call | solution.py:507
  41.7 1.6 %copy.10 = f32[80,512]{1,0:T(8,128)} copy(f32[80,512]{1,0:T(8,128)} %shard_map.82) | data formatting | bytes 327680

commit v5 on v4

--- a/solution.py
+++ b/solution.py
@@ -111,10 +111,10 @@
         copy.start()
         return copy
 
+    adjoint_copy = fetch(3, adjoint_in, adjoint_ref)
     list_copy = fetch(0, list_in, list_ref)
     cluster_copy = fetch(1, cluster_in, cluster_ref)
     k_copy = fetch(2, k_in, k_ref)
-    adjoint_copy = fetch(3, adjoint_in, adjoint_ref)
     scale_copy = fetch(4, scale_in, scale_ref)
     links_copy = fetch(5, links_in, links_ref)
     neighbour_copy = fetch(6, neighbour_in, neighbour_ref)
@@ -391,9 +391,9 @@
 
     first = LEVELS[0]
     placed = {first: place(first)}
-    predict(0)
     pl.semaphore_wait(barrier, sum(has.astype(jnp.int32) for has in has_target))
     each(has_target, lambda h: id_wave(first, h).start())
+    predict(0)
     send(0)
 
     for c in (1, 0):

time: 43.4 us -> 43.2 us (level)
  no operation moved by 1% of the time
where the time goes in v5:
time: 43.2 us; the launch traced here: 43.1 us
  Pallas kernels  41.5 us (96%)
  local copies, waits for them, and re-layouts  1.59 us (4%)
    pallas_call x1, Pallas kernels, shards(): pl.pallas_call(functools.partial(kernel, n_slab, n_sub), out_shape=jax.Sh...  41.5 us
    unnamed x1, local copies, waits for them, and re-layouts  1.59 us

profile of v5, /device:TPU:24, one launch (start us, length us, event | category | flops | bytes accessed | tf_op | source)
XLA Modules:
  0.0 43.1 jit_solution(2658873927969876370)
XLA Ops:
  0.0 41.5 %shard_map.82 = f32[80,512]{1,0:T(8,128)} custom-call(f32[80,512]{1,0:T(8,128)} %adjoint_in.1, f32[1,512]{1,0:T(1,128)} %bitcast.2, s32[1,512]{1,0:T(1,128)} %bitcast.3, s32[4,512]{1,0:T(4,128)} %links_in.1, s32[2,256]{1,0:T(2,128)} %list_in.1, f32[80,80]{1,0:T(8,128)} %k_in.1, f32[80,80]{1,0:T(8,128)} %self_in.1, f32[80,320]{1,0:T(8,128)} %neighbour_in.1), custom_call_target="tpu_custom_call" | custom-call | tf_op jit(solution)/shard_map/pallas_call | solution.py:507
  41.5 1.6 %copy.10 = f32[80,512]{1,0:T(8,128)} copy(f32[80,512]{1,0:T(8,128)} %shard_map.82) | data formatting | bytes 327680
